TPU v7x, 256 devices: a whole 4x4x8 slice. The times are simulated.
256 devices in a mesh: tm: 32 (over y_lo, z, core), stream: 8 (over y_hi, x).
Axes of the slice: x: 4, y: 4 (y_hi: 2, y_lo: 2; y = y_hi * 2 + y_lo), z: 8, core: 2. Of those that a mesh axis runs over, the one named last changes fastest.
Arguments:
- latents: bfloat16 [8, 8192, 512], P('stream', 'tm'), parts along dimension 0, may hold values from -6 to 6
- gain_attn: float32 [1, 512], replicated, may hold values from 0.5 to 1.5
- w_query: bfloat16 [1, 512, 512], replicated, may hold values from -8 to 8
- w_key: bfloat16 [1, 512, 512], replicated, may hold values from -8 to 8
- w_value: bfloat16 [1, 512, 512], replicated, may hold values from -0.25 to 0.25
- w_out: bfloat16 [1, 512, 512], replicated, may hold values from -0.25 to 0.25
- scale_attn: float32 [1, 512], replicated, may hold values from 0.3 to 1
- gain_ffn: float32 [1, 512], replicated, may hold values from 0.5 to 1.5
- w_up: bfloat16 [1, 512, 2048], replicated, may hold values from -0.25 to 0.25
- w_down: bfloat16 [1, 2048, 512], replicated, may hold values from -0.125 to 0.125
- scale_ffn: float32 [1, 512], replicated, may hold values from 0.3 to 1
- w_lift: bfloat16 [7, 512, 1024], P(None, None, 'tm'), may hold values from -0.09375 to 0.09375
- bias_lift: float32 [1024], replicated, may hold values from -2 to 2
- w_upsample: bfloat16 [1024, 8192], P(None, 'tm'), may hold values from -0.125 to 0.125
- bias_upsample: float32 [512], replicated, may hold values from -2 to 2
- w_conv_first: bfloat16 [512, 768], replicated, may hold values from -0.15625 to 0.15625
- bias_first: float32 [256], replicated, may hold values from -2 to 2
- w_conv_second: bfloat16 [256, 512], replicated, may hold values from -0.375 to 0.375
- bias_second: float32 [512], replicated, may hold values from -2 to 2
Outputs:
- audio_features: bfloat16 [8, 65536, 512], P('stream', 'tm'), parts along dimension 0
There are 8 independent parts, one for each index of `stream`. A program takes and returns all parts, laid end to end along the dimension named above; an argument that names none is the same for every part. Nothing has to cross between parts.
All inputs are finite; a program needn't handle non-finite values.
Results may differ from a plain program's by a relative error of at most 0.015.
Values may be sent and summed in bfloat16 or wider, within the bound.
A program may use at most 128 MiB of HBM per device.

v0:
```python
import jax
import jax.numpy as jnp
from jax import lax
from jax.sharding import PartitionSpec as P

HEADS = 8
HEAD_DIM = 64
WIN = 250
UPS = 8


def passed_along(block, axis, distance):
    devices = range(lax.axis_size(axis))
    route = [(i - distance, i) for i in devices if i - distance in devices]
    return lax.ppermute(block, axis, route)


def layer_norm(values_in, gain_row):
    average = jnp.mean(values_in, axis=-1, keepdims=True)
    centred = values_in - average
    variance = jnp.mean(centred * centred, axis=-1, keepdims=True)
    return centred * lax.rsqrt(variance + 1e-05) * gain_row


def rotate(tensor, positions):
    half_size = tensor.shape[-1] // 2
    frequency = jnp.exp(-jnp.log(10000.0) * jnp.arange(half_size, dtype=jnp.float32) / half_size)
    angles = positions.astype(jnp.float32)[:, None] * frequency[None, :]
    cosine = jnp.cos(angles)[:, None, :]
    sine_part = jnp.sin(angles)[:, None, :]
    front_half = tensor[..., :half_size]
    back_half = tensor[..., half_size:]
    return jnp.concatenate(
        [front_half * cosine - back_half * sine_part, front_half * sine_part + back_half * cosine],
        axis=-1,
    )


def heads_of(normed, weight, positions, rotated):
    projected = jnp.dot(normed, weight, preferred_element_type=jnp.float32)
    projected = projected.reshape(projected.shape[:-1] + (HEADS, HEAD_DIM))
    if rotated:
        projected = rotate(projected, positions)
    return projected.astype(jnp.bfloat16)


def attend(query_rows, key_rows, value_rows, query_pos, key_pos):
    scores = jnp.einsum(
        "sqhd,skhd->shqk", query_rows, key_rows, preferred_element_type=jnp.float32
    ) / jnp.sqrt(jnp.float32(HEAD_DIM))
    allowed = (
        (key_pos[None, :] <= query_pos[:, None])
        & (key_pos[None, :] > query_pos[:, None] - WIN)
        & (key_pos[None, :] >= 0)
    )
    scores = jnp.where(allowed, scores, -1e30)
    row_max = jnp.max(scores, axis=-1, keepdims=True)
    weights = jnp.where(allowed, jnp.exp(scores - row_max), 0.0)
    probs = (weights / jnp.sum(weights, axis=-1, keepdims=True)).astype(jnp.bfloat16)
    mixed = jnp.einsum("shqk,skhd->sqhd", probs, value_rows, preferred_element_type=jnp.float32)
    return mixed.astype(jnp.bfloat16)


def body(
    latents,
    gain_attn,
    w_query,
    w_key,
    w_value,
    w_out,
    scale_attn,
    gain_ffn,
    w_up,
    w_down,
    scale_ffn,
    w_lift,
    bias_lift,
    w_upsample,
    bias_upsample,
    w_conv_first,
    bias_first,
    w_conv_second,
    bias_second,
):
    streams, frames, model_width = latents.shape
    channels = bias_upsample.shape[0]
    inner_width = bias_first.shape[0]
    offset = lax.axis_index("tm") * frames
    local_pos = offset + jnp.arange(frames, dtype=jnp.int32)
    tail_pos = offset - WIN + jnp.arange(WIN, dtype=jnp.int32)
    key_pos = jnp.concatenate([tail_pos, local_pos])
    current = latents
    state = current.astype(jnp.float32)
    normed = layer_norm(state, gain_attn[0]).astype(jnp.bfloat16)
    query_rows = heads_of(normed, w_query[0], local_pos, True)
    key_rows = heads_of(normed, w_key[0], local_pos, True)
    value_rows = heads_of(normed, w_value[0], local_pos, False)
    key_tail, value_tail = passed_along((key_rows[:, -WIN:], value_rows[:, -WIN:]), "tm", 1)
    all_keys = jnp.concatenate([key_tail, key_rows], axis=1)
    all_values = jnp.concatenate([value_tail, value_rows], axis=1)
    mixed = attend(query_rows, all_keys, all_values, local_pos, key_pos).reshape(
        streams, frames, model_width
    )
    residual = state + scale_attn[0] * jnp.dot(mixed, w_out[0], preferred_element_type=jnp.float32)
    normed_two = layer_norm(residual, gain_ffn[0]).astype(jnp.bfloat16)
    hidden = jax.nn.gelu(
        jnp.dot(normed_two, w_up[0], preferred_element_type=jnp.float32), approximate=False
    ).astype(jnp.bfloat16)
    current = (
        residual + scale_ffn[0] * jnp.dot(hidden, w_down[0], preferred_element_type=jnp.float32)
    ).astype(jnp.bfloat16)
    prior_rows = passed_along(current[:, -6:], "tm", 1)
    extended_rows = jnp.concatenate([prior_rows, current], axis=1)
    lift_rows = extended_rows.shape[1] - 6
    piece = lax.all_gather(w_lift, "tm", axis=2, tiled=True)
    total = jnp.dot(extended_rows[:, 0:lift_rows], piece[0], preferred_element_type=jnp.float32)
    for tap_id in range(1, 7):
        total = total + jnp.dot(
            extended_rows[:, tap_id : tap_id + lift_rows],
            piece[tap_id],
            preferred_element_type=jnp.float32,
        )
    activated = jax.nn.elu(total + bias_lift).astype(jnp.bfloat16)
    prior_active = passed_along(activated[:, -2:], "tm", 1)
    active_rows = jnp.concatenate([prior_active, activated], axis=1)
    tap_all = jnp.dot(
        active_rows,
        lax.all_gather(w_upsample, "tm", axis=1, tiled=True),
        preferred_element_type=jnp.float32,
    )
    tap_all = tap_all.reshape(streams, active_rows.shape[1], 2, UPS, channels)
    upsampled = (
        (bias_upsample + tap_all[:, 2:, 0] + tap_all[:, 1:-1, 1])
        .reshape(streams, frames * UPS, channels)
        .astype(jnp.bfloat16)
    )
    rim_terms = bias_upsample + tap_all[:, 1, 0, UPS - 2 :] + tap_all[:, 0, 1, UPS - 2 :]
    rim_rows = jnp.where(lax.axis_index("tm") > 0, rim_terms, 0.0).astype(jnp.bfloat16)
    extended = jnp.concatenate([rim_rows, upsampled], axis=1)
    rectified = jax.nn.elu(extended.astype(jnp.float32)).astype(jnp.bfloat16)
    conv_terms = jnp.dot(rectified, w_conv_first, preferred_element_type=jnp.float32).reshape(
        streams, frames * UPS + 2, 3, inner_width
    )
    squeezed = jax.nn.elu(
        bias_first + conv_terms[:, :-2, 0] + conv_terms[:, 1:-1, 1] + conv_terms[:, 2:, 2]
    ).astype(jnp.bfloat16)
    output = (
        upsampled.astype(jnp.float32)
        + bias_second
        + jnp.dot(squeezed, w_conv_second, preferred_element_type=jnp.float32)
    )
    return output.astype(jnp.bfloat16)


def solution(mesh):
    placed = (
        P("stream", "tm", None),
        P(),
        P(),
        P(),
        P(),
        P(),
        P(),
        P(),
        P(),
        P(),
        P(),
        P(None, None, "tm"),
        P(),
        P(None, "tm"),
        P(),
        P(),
        P(),
        P(),
        P(),
    )
    return jax.shard_map(
        body, mesh=mesh, in_specs=placed, out_specs=P("stream", "tm", None), check_vma=False
    )
```

profile of v0, /device:TPU:1, one launch (start us, length us, event | category | flops | bytes accessed | tf_op | source)
XLA Modules:
  0.0 276.3 jit_solution(16938871521497050690)
XLA Ops:
  6.5 0.7 all-gather.3.cloned.1.call-update
  7.3 0.7 all-gather.5.cloned.1.call-update
  8.0 1.3 copy.27
  9.3 1.3 copy.28
  10.6 0.1 convert_reduce_fusion
  10.7 0.2 fusion.100
  10.9 0.4 convolution_bitcast_fusion.3
  11.4 0.4 convolution_bitcast_fusion.2
  11.8 0.2 multiply_cosine_fusion
  12.0 0.2 fusion.153
  12.1 0.8 pad_maximum_fusion.1
  13.0 4.9 %collective-permute-start.1 = (bf16[1,250,8,64]{1,3,2,0:T(8,128)(2,1)}, bf16[1,250,8,64]{1,3,2,0:T(8,128)(2,1)}, u32[]{:S(2)}, u32[]{:S(2)}) collective-permute-start(bf16[1,250,8,64]{1,3,2,0:T(8,128)(2,1)} %pad_maximum_fusion.1), channel_id=1, source_target_pairs={{0,8},{8,16},{16,24},{24,32},{32,40},{40,48},{48,56},{56,64},{64,7... | collective-permute-start | bytes 768008 | tf_op jit(solution)/shard_map/ppermute | solution.py:15
  17.9 1.3 copy.26
  19.2 0.4 fusion.52
  19.6 0.7 copy-done.6
  20.3 0.1 slice.112
  20.5 2.1 collective-permute-start
  22.6 0.1 pad_add_fusion
  22.7 0.1 broadcast_compare_fusion
  22.8 0.2 and_and_fusion
  23.0 1.7 fusion.105
  24.7 2.8 fusion.210
  27.5 0.9 fusion.51
  28.5 0.1 copy-done.5
  28.5 0.4 fusion.211
  29.0 0.2 multiply_reduce_fusion
  29.2 7.2 %fusion.48 = bf16[1,256,512]{2,1,0:T(8,128)(2,1)S(1)} fusion(f32[1,256,512]{2,1,0:T(8,128)S(1)} %get-tuple-element.20, bf16[1,2048,512]{2,1,0:T(8,128)(2,1)S(1)} %copy-done, bf16[1,512,2048]{2,1,0:T(8,128)(2,1)} %param.27, f32[512]{0:T(512)S(1)} %bitcast.209, f32[256]{0:T(256)S(1)} %add_rsqrt_fusion, f32[256]{0:T(256)S(1)} %broadcast_multiply_fusion, ...), kind=kOutput, calls=%fused_computation.75 | convolution fusion | flops 1108738048 | bytes 4986880 | tf_op jit(solution)/shard_map/dot_general | solution.py:110
  36.4 4.1 %collective-permute-start.2 = (bf16[1,6,512]{2,1,0:T(8,128)(2,1)S(1)}, bf16[1,6,512]{2,1,0:T(8,128)(2,1)S(1)}, u32[]{:S(2)}, u32[]{:S(2)}) collective-permute-start(bf16[1,6,512]{2,1,0:T(8,128)(2,1)S(1)} %slice.117), channel_id=1, source_target_pairs={{0,8},{8,16},{16,24},{24,32},{32,40},{40,48},{48,56},{56,64},{64,7... | collective-permute-start | bytes 18440 | tf_op jit(solution)/shard_map/ppermute | solution.py:15
  40.6 0.6 collective-permute-done.2
  41.1 43.8 %all-gather.3.cloned.1.call-done = bf16[7,512,1024]{1,2,0:T(8,128)(2,1)} async-done(((bf16[7,512,32]{1,2,0:T(8,128)(2,1)}), bf16[7,512,1024]{1,2,0:T(8,128)(2,1)}) %all-gather.3.cloned.1.call-update) | async-done | bytes 7340048 | tf_op jit(solution)/shard_map/all_gather | solution.py:115
  84.9 1.8 fusion.63
  86.8 2.1 fusion.62
  88.9 1.7 convolution_add_fusion.4
  90.6 0.5 convolution_add_fusion.3
  91.1 0.5 convolution_add_fusion.2
  91.6 0.5 convolution_add_fusion.1
  92.1 0.2 copy-done.12
  92.3 0.8 fusion.61
  93.1 3.2 %collective-permute-start.3 = (bf16[1,2,1024]{2,1,0:T(2,128)(2,1)S(1)}, bf16[1,2,1024]{2,1,0:T(2,128)(2,1)S(1)}, u32[]{:S(2)}, u32[]{:S(2)}) collective-permute-start(bf16[1,2,1024]{2,1,0:T(2,128)(2,1)S(1)} %slice.135), channel_id=1, source_target_pairs={{0,8},{8,16},{16,24},{24,32},{32,40},{40,48},{48,56},{56,64},{64,7... | collective-permute-start | bytes 12296 | tf_op jit(solution)/shard_map/ppermute | solution.py:15
  96.3 0.3 copy.33
  96.5 114.5 %all-gather.5.cloned.1.call-done = bf16[1024,8192]{1,0:T(8,128)(2,1)} async-done(((bf16[1024,256]{1,0:T(8,128)(2,1)}), bf16[1024,8192]{1,0:T(8,128)(2,1)}) %all-gather.5.cloned.1.call-update) | async-done | bytes 16777232 | tf_op jit(solution)/shard_map/all_gather | solution.py:128
  211.1 22.4 %copy.29 = bf16[8192,1024]{1,0:T(8,128)(2,1)} copy(bf16[8192,1024]{0,1:T(8,128)(2,1)} %bitcast.198) | data formatting | bytes 33554432 | tf_op jit(solution)/shard_map/dot_general | solution.py:126
  233.5 19.1 %convolution_bitcast_fusion.1 = f32[1,258,2,8,512]{4,1,3,2,0:T(8,128)} fusion(bf16[2,8,512,1024]{3,2,1,0:T(8,128)(2,1)} %bitcast.199, bf16[1,256,1024]{2,1,0:T(8,128)(2,1)S(1)} %fusion.61, bf16[1,2,1024]{2,1,0:T(2,128)(2,1)S(1)} %collective-permute-done.3), kind=kOutput, calls=%fused_computation.17 | convolution fusion | flops 4329578496 | bytes 25759744 | tf_op jit(solution)/shard_map/dot_general | solution.py:126
  252.6 4.6 %fusion.209 = (f32[1,256,1,8,512]{4,1,3,2,0:T(8,128)S(1)}, f32[1,256,1,8,512]{4,1,3,2,0:T(8,128)S(1)}) fusion(f32[1,258,2,8,512]{4,1,3,2,0:T(8,128)} %convolution_bitcast_fusion.1), kind=kLoop, calls=%fused_computation.253 | loop fusion | bytes 16777216 | tf_op jit(solution)/shard_map/slice | solution.py:133
  257.3 0.8 fusion.208
  258.1 4.8 %fusion.3 = bf16[2048,512]{1,0:T(8,128)(2,1)S(1)} fusion(f32[1,256,1,8,512]{4,1,3,2,0:T(8,128)S(1)} %get-tuple-element.8, f32[1,256,1,8,512]{4,1,3,2,0:T(8,128)S(1)} %get-tuple-element.7, f32[512]{0:T(512)S(1)} %copy-done.9), kind=kLoop, calls=%fused_computation.9 | loop fusion | flops 3145728 | bytes 10487808 | tf_op jit(solution)/shard_map/convert_element_type | solution.py:135
  262.9 3.4 %convolution_bitcast_fusion = f32[1,2050,3,256]{3,1,2,0:T(8,128)S(1)} fusion(bf16[3,256,512]{2,1,0:T(8,128)(2,1)S(1)} %bitcast.202, bf16[2048,512]{1,0:T(8,128)(2,1)S(1)} %fusion.3, bf16[2,512]{1,0:T(2,128)(2,1)S(1)} %fusion.158), kind=kOutput, calls=%fused_computation.5 | convolution fusion | flops 1620582400 | bytes 9183232 | tf_op jit(solution)/shard_map/dot_general | solution.py:141
  266.3 3.1 %fusion.5 = bf16[1,2048,512]{2,1,0:T(8,128)(2,1)} fusion(bf16[256,512]{1,0:T(8,128)(2,1)S(1)} %copy-done.11, bf16[2048,512]{1,0:T(8,128)(2,1)S(1)} %fusion.3, f32[512]{0:T(512)S(1)} %copy-done.15, f32[1,2050,3,256]{3,1,2,0:T(8,128)S(1)} %convolution_bitcast_fusion, f32[256]{0:T(256)S(1)} %copy-done.16), kind=kOutput, calls=%fused_computation.20 | convolution fusion | flops 544735232 | bytes 10750976 | tf_op jit(solution)/shard_map/dot_general | solution.py:150
  (47 shorter events, 0.2 us)
Async XLA Ops:
  6.5 22.6 %copy-start = (bf16[1,2048,512]{2,1,0:T(8,128)(2,1)S(1)}, bf16[1,2048,512]{2,1,0:T(8,128)(2,1)}, u32[]{:S(2)}) copy-start(bf16[1,2048,512]{2,1,0:T(8,128)(2,1)} %param.28) | copy-start | bytes 6291460
  6.5 4.0 %copy-start.2 = (bf16[1,256,512]{2,1,0:T(8,128)(2,1)S(1)}, bf16[1,256,512]{2,1,0:T(8,128)(2,1)}, u32[]{:S(2)}) copy-start(bf16[1,256,512]{2,1,0:T(8,128)(2,1)} %param.19) | copy-start | bytes 786436
  6.5 4.4 %copy-start.8 = (f32[1,512]{1,0:T(1,128)S(1)}, f32[1,512]{1,0:T(1,128)}, u32[]{:S(2)}) copy-start(f32[1,512]{1,0:T(1,128)} %param.20) | copy-start | bytes 6148
  6.5 78.4 %all-gather.3.cloned.1.call-start = ((), (), s32[]{:S(2)}) async-start(), calls=%async_computation | async-start | bytes 7569408 | tf_op jit(solution)/shard_map/all_gather | solution.py:115
  7.3 203.8 %all-gather.5.cloned.1.call-start = ((), (), s32[]{:S(2)}) async-start(), calls=%async_computation.1 | async-start | bytes 17301504 | tf_op jit(solution)/shard_map/all_gather | solution.py:128
  13.0 10.0 %collective-permute-start.1 = (bf16[1,250,8,64]{1,3,2,0:T(8,128)(2,1)}, bf16[1,250,8,64]{1,3,2,0:T(8,128)(2,1)}, u32[]{:S(2)}, u32[]{:S(2)}) collective-permute-start(bf16[1,250,8,64]{1,3,2,0:T(8,128)(2,1)} %pad_maximum_fusion.1), channel_id=1, source_target_pairs={{0,8},{8,16},{16,24},{24,32},{32,40},{40,48},{48,56},{56,64},{64,7... | collective-permute-start | bytes 768008 | tf_op jit(solution)/shard_map/ppermute | solution.py:15
  19.6 0.7 copy-start.6
  20.5 7.0 %collective-permute-start = (bf16[1,250,8,64]{1,3,2,0:T(8,128)(2,1)S(1)}, bf16[1,250,8,64]{1,3,2,0:T(8,128)(2,1)S(1)}, u32[]{:S(2)}, u32[]{:S(2)}) collective-permute-start(bf16[1,250,8,64]{1,3,2,0:T(8,128)(2,1)S(1)} %slice.112), channel_id=1, source_target_pairs={{0,8},{8,16},{16,24},{24,32},{32,40},{40,48},{48,56},{56,64},{64,7... | collective-permute-start | bytes 768008 | tf_op jit(solution)/shard_map/ppermute | solution.py:15
  24.7 2.8 %copy-start.7 = (bf16[1,256,8,64]{1,3,2,0:T(8,128)(2,1)S(1)}, bf16[1,256,8,64]{1,3,2,0:T(8,128)(2,1)}, u32[]{:S(2)}) copy-start(bf16[1,256,8,64]{1,3,2,0:T(8,128)(2,1)} %copy-done.6) | copy-start | bytes 786436
  27.5 1.1 copy-start.5
  27.5 1.0 copy-start.10
  28.4 0.8 copy-start.13
  28.4 0.8 copy-start.14
  36.4 4.7 %collective-permute-start.2 = (bf16[1,6,512]{2,1,0:T(8,128)(2,1)S(1)}, bf16[1,6,512]{2,1,0:T(8,128)(2,1)S(1)}, u32[]{:S(2)}, u32[]{:S(2)}) collective-permute-start(bf16[1,6,512]{2,1,0:T(8,128)(2,1)S(1)} %slice.117), channel_id=1, source_target_pairs={{0,8},{8,16},{16,24},{24,32},{32,40},{40,48},{48,56},{56,64},{64,7... | collective-permute-start | bytes 18440 | tf_op jit(solution)/shard_map/ppermute | solution.py:15
  84.9 5.7 %copy-start.3 = (bf16[7,512,1024]{1,2,0:T(8,128)(2,1)S(1)}, bf16[7,512,1024]{1,2,0:T(8,128)(2,1)}, u32[]{:S(2)}) copy-start(bf16[7,512,1024]{1,2,0:T(8,128)(2,1)} %all-gather.3.cloned.1.call-done) | copy-start | bytes 22020100
  91.6 0.7 copy-start.12
  92.3 4.0 %copy-start.4 = (bf16[512,768]{1,0:T(8,128)(2,1)S(1)}, bf16[512,768]{1,0:T(8,128)(2,1)}, u32[]{:S(2)}) copy-start(bf16[512,768]{1,0:T(8,128)(2,1)} %param.34) | copy-start | bytes 2359300
  93.1 140.4 %collective-permute-start.3 = (bf16[1,2,1024]{2,1,0:T(2,128)(2,1)S(1)}, bf16[1,2,1024]{2,1,0:T(2,128)(2,1)S(1)}, u32[]{:S(2)}, u32[]{:S(2)}) collective-permute-start(bf16[1,2,1024]{2,1,0:T(2,128)(2,1)S(1)} %slice.135), channel_id=1, source_target_pairs={{0,8},{8,16},{16,24},{24,32},{32,40},{40,48},{48,56},{56,64},{64,7... | collective-permute-start | bytes 12296 | tf_op jit(solution)/shard_map/ppermute | solution.py:15
  252.6 5.4 %copy-start.9 = (f32[512]{0:T(512)S(1)}, f32[512]{0:T(512)}, u32[]{:S(2)}) copy-start(f32[512]{0:T(512)} %param.33) | copy-start | bytes 6148
  262.9 3.4 %copy-start.11 = (bf16[256,512]{1,0:T(8,128)(2,1)S(1)}, bf16[256,512]{1,0:T(8,128)(2,1)}, u32[]{:S(2)}) copy-start(bf16[256,512]{1,0:T(8,128)(2,1)} %param.36) | copy-start | bytes 786436
  262.9 3.4 %copy-start.15 = (f32[512]{0:T(512)S(1)}, f32[512]{0:T(512)}, u32[]{:S(2)}) copy-start(f32[512]{0:T(512)} %param.37) | copy-start | bytes 6148
  262.9 3.4 %copy-start.16 = (f32[256]{0:T(256)S(1)}, f32[256]{0:T(256)}, u32[]{:S(2)}) copy-start(f32[256]{0:T(256)} %param.35) | copy-start | bytes 3076
  266.3 3.2 %copy-start.1 = (bf16[1,2048,512]{2,1,0:T(8,128)(2,1)S(1)}, bf16[1,2048,512]{2,1,0:T(8,128)(2,1)}, u32[]{:S(2)}) copy-start(bf16[1,2048,512]{2,1,0:T(8,128)(2,1)} %param.28) | copy-start | bytes 6291460
Sparse Core Ops, SparseCore 0:
  9.2 75.6 all-gather.2
  86.7 124.3 all-gather.4
where the time goes:
time: 277 us; the launch traced here: 276 us
  waiting for transfers between devices  160 us (58%)
  matrix products  45 us (16%)
  local copies, waits for them, and re-layouts  33.1 us (12%)
  starting transfers between devices  14.4 us (5%)
  between operations  13.9 us (5%)
  other arithmetic  9.67 us (3%)
    all_gather x1, waiting for transfers between devices, body(): lax.all_gather(w_upsample, 'tm', axis=1, tiled=True)  115 us
    all_gather x1, waiting for transfers between devices, body(): piece = lax.all_gather(w_lift, 'tm', axis=2, tiled=True)  43.8 us
    dot_general x1, local copies, waits for them, and re-layouts, body(): jnp.dot(active_rows, lax.all_gather(w_upsample, 'tm', axis=1, tiled=True)...  22.4 us
    dot_general x1, matrix products, body(): jnp.dot(active_rows, lax.all_gather(w_upsample, 'tm', axis=1, tiled=True)...  19.1 us
    ppermute x4, starting transfers between devices, passed_along(): return lax.ppermute(block, axis, route)  14.3 us
    dot_general x1, matrix products, body(): jnp.dot(hidden, w_down[0], preferred_element_type=jnp.float32)  7.18 us
    dot_general x6, matrix products, body(): jnp.dot(extended_rows[:, tap_id:tap_id + lift_rows], piece[tap_id], prefe...  6.18 us
  transfers between devices with their start and end apart: 6, of which 3 were waited for; matrix products, arithmetic and copies ran while one was open for 18% of the time, Pallas kernels for 0%

commit v1 on v0

v1 whole, which is shorter than its diff:
```python
import functools
import math

import jax
import jax.numpy as jnp
import numpy as np
from jax import lax
from jax.experimental import pallas as pl
from jax.experimental.pallas import tpu as pltpu
from jax.sharding import PartitionSpec as P

MESH = pl.DeviceIdType.MESH
BF16, F32 = jnp.bfloat16, jnp.float32
HEADS, HEAD_DIM, WIN, UPS = 8, 64, 250, 8
FRAMES, D, FF, C0, C1, CH = 256, 512, 2048, 1024, 512, 256
HALO = 272
ROWS = HALO + FRAMES
LIVE = 272
LEAD = LIVE - FRAMES


def coords():
    t = lax.axis_index("tm")
    s = lax.axis_index("stream")
    return s % 4, (s // 4) * 2 + t // 16, (t // 2) % 8, t % 2


def device(x, y, z, c):
    return ((y % 2) * 16 + z * 2 + c, (y // 2) * 4 + x)


class Gather:
    def __init__(self, wl, wu, lbuf, ubuf, send_sems, recv_sems):
        self.x, self.y, self.z, self.c = x, y, z, c = coords()
        self.xp = self.x % 2
        self.src = {"L": wl, "U": wu}
        self.buf = {"L": lbuf, "U": ubuf}
        self.send_sems, self.recv_sems = send_sems, recv_sems
        self.sent = []
        self.to = {
            "z+": device(x, y, (z + 1) % 8, c),
            "z-": device(x, y, (z + 7) % 8, c),
            "y+": device(x, (y + 1) % 4, z, c),
            "y-": device(x, (y + 3) % 4, z, c),
            "x+": device((x + 1) % 4, y, z, c),
            "x-": device((x + 3) % 4, y, z, c),
            "s": device(x, y, z, 1 - c),
        }
        t, s = lax.axis_index("tm"), lax.axis_index("stream")
        self.after = [((t + k) % 32, s) for k in (1, 2)]
        self.before = [((t + 32 - k) % 32, s) for k in (1, 2)]

    def span(self, kind, part):
        xp = self.xp
        if kind == "L":
            return {
                "W": (0, 7),
                "P": (2 * xp, 5),
                "P0": (2 * xp, 3),
                "P1": (2 * xp + 3, 2),
                "M": (5 * xp, 2),
                "O": (5 - 5 * xp, 2),
            }[part]
        start, size = {
            "W": (0, 1024),
            "P": (336 * xp, 688),
            "P0": (336 * xp, 352),
            "P1": (336 * xp + 352, 336),
            "M": (688 * xp, 336),
            "O": (688 - 688 * xp, 336),
        }[part]
        return (start if isinstance(start, int) else pl.multiple_of(start, 16)), size

    def ref(self, kind, row, d, part, core=None, own=False):
        start, size = self.span(kind, part)
        if own:
            return self.src[kind].at[pl.ds(start, size)]
        yl, zz = (self.y + row) % 2, (self.z + d + 8) % 8
        core = self.c if core is None else core
        if kind == "U":
            return self.buf[kind].at[yl, zz, core, pl.ds(start, size)]
        first = pl.multiple_of(32 * (yl * 16 + zz * 2 + core), 32)
        return self.buf[kind].at[pl.ds(start, size), pl.ds(first, 32)]

    def start(self, src, dst, target, recv):
        copy = pltpu.make_async_remote_copy(
            src_ref=src,
            dst_ref=dst,
            send_sem=self.send_sems.at[len(self.sent)],
            recv_sem=self.recv_sems.at[recv],
            device_id=target,
            device_id_type=MESH,
        )
        copy.start()
        self.sent.append(copy)

    def send(self, kind, row, d, part, where, recv):
        src = self.ref(kind, row, d, part, own=row == 0 and d == 0)
        self.start(src, self.ref(kind, row, d, part), self.to[where], recv)

    def wait(self, ref, recv):
        pltpu.make_async_remote_copy(
            src_ref=ref,
            dst_ref=ref,
            send_sem=self.send_sems.at[0],
            recv_sem=self.recv_sems.at[recv],
            device_id=self.to["s"],
            device_id_type=MESH,
        ).wait_recv()

    def wait_part(self, kind, row, d, part, recv, core=None):
        self.wait(self.ref(kind, row, d, part, core=core), recv)

    @staticmethod
    def sem(what, kind, row, d):
        base = 50 * (kind == "U")
        if what == "P1":
            return base + 48 + row
        return base + {"P": 0, "O": 16, "S": 32}[what] + row * 8 + d + 3

    def part_p(self, kind, row, d):
        sem = self.sem
        if row or d:
            if (row, d) in ((0, 4), (1, 0)):
                self.wait_part(kind, row, d, "P0", sem("P", kind, row, d))
                self.wait_part(kind, row, d, "P1", sem("P1", kind, row, d))
            else:
                self.wait_part(kind, row, d, "P", sem("P", kind, row, d))
        if row == 0:
            if d in (0, -1, -2):
                self.send(kind, 0, d, "P", "z+", sem("P", kind, 0, d - 1))
            if d in (0, 1, 2):
                self.send(kind, 0, d, "P", "z-", sem("P", kind, 0, d + 1))
            if d == -3:
                self.send(kind, 0, d, "P0", "z+", sem("P", kind, 0, 4))
            if d == 3:
                self.send(kind, 0, d, "P1", "z-", sem("P1", kind, 0, 4))
            if d == 0:
                self.send(kind, 0, 0, "P0", "y+", sem("P", kind, 1, 0))
                self.send(kind, 0, 0, "P1", "y-", sem("P1", kind, 1, 0))
                self.send(kind, 0, 0, "W", "s", sem("S", kind, 0, 0))
            else:
                self.send(kind, 0, d, "P", "y+" if d in (1, -2, 3) else "y-", sem("P", kind, 1, d))
        if row or d:
            self.send(kind, row, d, "M", "x+" if (d + row) % 2 else "x-", sem("O", kind, row, d))

    def part_o(self, kind, row, d):
        if row or d:
            self.wait_part(kind, row, d, "O", self.sem("O", kind, row, d))
            self.send(kind, row, d, "W", "s", self.sem("S", kind, row, d))

    def from_other_core(self, kind, row, d):
        self.wait_part(kind, row, d, "W", self.sem("S", kind, row, d), core=1 - self.c)

    def barrier(self):
        semaphore = pltpu.get_barrier_semaphore()
        targets = list(self.to.values()) + self.before
        for target in targets:
            pl.semaphore_signal(semaphore, inc=1, device_id=target, device_id_type=MESH)
        pl.semaphore_wait(semaphore, len(targets))

    def finish(self):
        for copy in self.sent:
            copy.wait_send()


def dot(a, b):
    return jnp.dot(a, b, preferred_element_type=F32)


def dot_nt(a, b):
    return lax.dot_general(a, b, (((1,), (1,)), ((), ())), preferred_element_type=F32)


def elu(v):
    return jnp.where(v > 0, v, jnp.exp(jnp.minimum(v, 0.0)) - 1.0)


def layer_norm(v, gain):
    centred = v - jnp.mean(v, axis=-1, keepdims=True)
    variance = jnp.mean(centred * centred, axis=-1, keepdims=True)
    return centred * lax.rsqrt(variance + 1e-05) * gain


def kernel(
    lat, ga, wq, wk, wv, wo, sa, gf, wup, wdn, sf, wl, bl, wu, bu, wc1, b1, wc2, b2, near, far,
    out,
    lbuf, ubuf, xin, vproj, vup, vdn, vc1, vc2, vga, vsa, vgf, vsf, vbl, vbu, vb1, vb2, vnear, vfar,
    qs, ks, vs, mixed, res, nrm, ffacc, cur7, act2, rect, summed, obf,
    send_sems, recv_sems, here_sems, out_sems,
):
    g = Gather(wl, wu, lbuf, ubuf, send_sems, recv_sems)
    t = lax.axis_index("tm")
    here = []

    def bring(src, dst):
        copy = pltpu.make_async_copy(src, dst, here_sems.at[len(here)])
        copy.start()
        here.append(copy)
        return copy

    own_x = bring(lat, xin.at[pl.ds(HALO, FRAMES)])
    g.barrier()
    g.start(lat, xin.at[pl.ds(LEAD, FRAMES)], g.after[0], 100)
    g.start(lat.at[pl.ds(FRAMES - LEAD, LEAD)], xin.at[pl.ds(0, LEAD)], g.after[1], 101)
    g.part_p("L", 0, 0)
    in_ga, in_near, in_far = bring(ga, vga), bring(near, vnear), bring(far, vfar)
    in_proj = [bring(w, vproj.at[i]) for i, w in enumerate((wk, wv, wq, wo))]
    g.part_p("U", 0, 0)
    own_l = bring(wl, g.ref("L", 0, 0, "W"))
    own_u = bring(wu, g.ref("U", 0, 0, "W"))
    in_up, in_dn = bring(wup, vup), bring(wdn, vdn)
    in_vec = [
        bring(a, b)
        for a, b in ((sa, vsa), (gf, vgf), (sf, vsf), (bl, vbl), (bu, vbu), (b1, vb1), (b2, vb2))
    ]
    in_c1, in_c2 = bring(wc1, vc1), bring(wc2, vc2)

    def keys_and_queries():
        own_x.wait()
        g.wait(xin.at[pl.ds(LEAD, FRAMES)], 100)
        g.wait(xin.at[pl.ds(0, LEAD)], 101)
        for copy in (in_ga, in_near, in_far, *in_proj):
            copy.wait()
        x = xin[...].astype(F32)
        normed = layer_norm(x, vga[...]).astype(BF16)
        cos_a, sin_a = vfar[0, pl.ds(t, 1), :], vfar[1, pl.ds(t, 1), :]
        cos_b, sin_b = vnear[0], vnear[1]
        cosine, sine = cos_a * cos_b - sin_a * sin_b, sin_a * cos_b + cos_a * sin_b
        lane = lax.broadcasted_iota(jnp.int32, (1, 128), 1)
        first = lane % 64 < 32
        sine = jnp.where(first, -sine, sine)

        def rope(v, cosine, sine):
            parts = []
            for i in range(4):
                block = v[:, 128 * i : 128 * i + 128]
                other = jnp.where(first, pltpu.roll(block, 96, 1), pltpu.roll(block, 32, 1))
                parts.append(block * cosine + other * sine)
            return jnp.concatenate(parts, axis=1).astype(BF16)

        ks[...] = rope(dot(normed, vproj[0]), cosine, sine)
        vs[...] = dot(normed, vproj[1]).astype(BF16)
        tail = ROWS - LIVE
        qs[...] = rope(dot(normed[tail:], vproj[2]), cosine[tail:], sine[tail:]) * BF16(0.125)

    def attention(pair):
        lanes = slice(128 * pair, 128 * pair + 128)
        low = lax.broadcasted_iota(jnp.int32, (1, 128), 1) < 64
        for q0, size, k0, width in ((256, 96, 0, 352), (352, 96, 96, 352), (448, 80, 192, 336)):
            q_row = q0 + lax.broadcasted_iota(jnp.int32, (size, width), 0)
            k_row = k0 + lax.broadcasted_iota(jnp.int32, (size, width), 1)
            allowed = (k_row <= q_row) & (k_row > q_row - WIN) & (k_row >= HALO - FRAMES * t)
            q = qs[q0 - 256 : q0 - 256 + size, lanes]
            k, v = ks[k0 : k0 + width, lanes], vs[k0 : k0 + width, lanes]
            halves = []
            for mask in (low, ~low):
                scores = jnp.where(allowed, dot_nt(jnp.where(mask, q, BF16(0)), k), -1e30)
                weights = jnp.exp(scores - jnp.max(scores, axis=-1, keepdims=True))
                weights = jnp.where(allowed, weights, 0.0)
                total = jnp.maximum(jnp.sum(weights, axis=-1, keepdims=True), 0.5)
                halves.append(dot((weights / total).astype(BF16), v))
            mixed[q0 - 256 : q0 - 256 + size, lanes] = jnp.where(low, *halves).astype(BF16)

    def after_attention():
        for copy in in_vec:
            copy.wait()
        state = xin[ROWS - LIVE :, :].astype(F32)
        residual = state + vsa[...] * dot(mixed[...], vproj[3])
        res[...] = residual
        nrm[...] = layer_norm(residual, vgf[...]).astype(BF16)
        in_up.wait()
        in_dn.wait()

    def feed_forward(i):
        cols = slice(512 * i, 512 * i + 512)
        v = dot(nrm[...], vup[:, cols])
        hidden = (0.5 * v * (1.0 + lax.erf(v * (1.0 / math.sqrt(2.0))))).astype(BF16)
        part = dot(hidden, vdn[cols, :])
        ffacc[...] = part if i == 0 else ffacc[...] + part

    live_row = lax.broadcasted_iota(jnp.int32, (LIVE, 1), 0)
    real = (live_row >= LEAD) | (t > 0)

    def layer_end():
        current = (res[...] + vsf[...] * ffacc[...]).astype(BF16).astype(F32)
        current = jnp.where(real, current, 0.0)
        for m in range(7):
            moved = pltpu.roll(current, 6 - m, 0) if m < 6 else current
            cur7[:, 512 * m : 512 * m + 512] = moved.astype(BF16)

    def lift(i):
        cols = slice(256 * i, 256 * i + 256)
        total = vbl[:, cols]
        for m in range(7):
            total = total + dot_nt(cur7[:, 512 * m : 512 * m + 512], lbuf[m, cols, :])
        active = jnp.where(real, elu(total), 0.0).astype(BF16)
        act2[:, cols] = active
        act2[:, C0 + 256 * i : C0 + 256 * i + 256] = pltpu.roll(active.astype(F32), 1, 0).astype(BF16)

    def upsample(d):
        j = (g.z + d + 8) % 8
        halves = []
        for half in range(2):
            cols = slice(256 * half, 256 * half + 256)
            up = dot(act2[:, :C0], ubuf[0, j, half]) + dot(act2[:, C0:], ubuf[1, j, half])
            up = (up + vbu[:, cols]).astype(BF16).astype(F32)
            halves.append(up)
        up = jnp.concatenate(halves, axis=1)
        kept = up[LEAD:] + vb2[...]
        for i in range(4):
            summed[i, pl.ds(j, FRAMES, stride=UPS), :] = kept[:, 128 * i : 128 * i + 128]
        rectified = jnp.where(real, elu(up), 0.0)
        rect[j + 2] = rectified.astype(BF16)

        @pl.when(j >= 6)
        def _():
            rect[j - 6] = pltpu.roll(rectified, 1, 0).astype(BF16)

    def residual_unit(d):
        j = (g.z + d + 8) % 8
        total = vb1[...]
        for m in range(3):
            total = total + dot(rect[j + m, LEAD:], vc1[:, CH * m : CH * m + CH])
        second = dot(elu(total).astype(BF16), vc2[...])
        rows = pl.ds(j, FRAMES, stride=UPS)
        for i in range(4):
            summed[i, rows, :] = summed[i, rows, :] + second[:, 128 * i : 128 * i + 128]

    def p(kind, row, *ds):
        for d in ds:
            g.part_p(kind, row, d)

    def o(kind, *ds, rows=(0, 1)):
        for d in ds:
            for row in rows:
                g.part_o(kind, row, d)

    def whole(kind, *ds):
        for d in ds:
            for row in (0, 1):
                g.from_other_core(kind, row, d)

    keys_and_queries()
    p("L", 0, -1, 1)
    p("L", 1, 0)
    attention(0)
    attention(1)
    p("L", 0, -2, 2)
    p("L", 1, -1, 1)
    o("L", 0, rows=(1,))
    attention(2)
    attention(3)
    p("U", 0, -1, 1)
    p("U", 1, 0)
    p("L", 0, -3, 3)
    p("L", 1, -2, 2)
    o("L", -1, 1)
    after_attention()
    feed_forward(0)
    feed_forward(1)
    p("L", 0, 4)
    p("L", 1, -3, 3)
    o("L", -2, 2)
    feed_forward(2)
    feed_forward(3)
    p("U", 0, -2, 2)
    p("U", 1, -1, 1)
    o("U", 0, rows=(1,))
    p("L", 1, 4)
    o("L", -3, 3)
    layer_end()
    o("L", 4)
    whole("L", 0, -1, 1, -2, 2, -3, 3, 4)
    own_l.wait()
    for i in range(4):
        lift(i)
    p("U", 0, -3, 3)
    p("U", 1, -2, 2)
    o("U", -1, 1)
    own_u.wait()
    for copy in (in_c1, in_c2):
        copy.wait()
    whole("U", 0)
    upsample(0)
    whole("U", -1, 1)
    p("U", 0, 4)
    p("U", 1, -3, 3)
    o("U", -2, 2)
    upsample(-1)
    upsample(1)
    residual_unit(1)
    p("U", 1, 4)
    o("U", -3, 3)
    whole("U", -2, 2)
    upsample(-2)
    upsample(2)
    residual_unit(0)
    residual_unit(2)
    o("U", 4)
    whole("U", -3, 3)
    upsample(-3)
    upsample(3)
    residual_unit(-1)
    residual_unit(3)
    whole("U", 4)
    upsample(4)
    residual_unit(4)
    residual_unit(-2)
    residual_unit(-3)
    leaving = []
    for i in range(4):
        rows = pl.ds(512 * i, 512)
        for k in range(4):
            obf[rows, 128 * k : 128 * k + 128] = summed[k, rows, :].astype(BF16)
        copy = pltpu.make_async_copy(obf.at[rows], out.at[rows], out_sems.at[i])
        copy.start()
        leaving.append(copy)
    for copy in leaving:
        copy.wait()

    g.finish()


def tables():
    frequency = 10000.0 ** (-np.arange(32, dtype=np.float64) / 32)
    frequency = np.tile(frequency, 4)[None, :]

    def both(frames):
        angles = frames[:, None] * frequency
        return np.stack([np.cos(angles), np.sin(angles)]).astype(np.float32)

    return both(np.arange(ROWS) - float(HALO)), both(np.arange(32) * float(FRAMES))


def body(
    latents, gain_attn, w_query, w_key, w_value, w_out, scale_attn, gain_ffn, w_up, w_down, scale_ffn,
    w_lift, bias_lift, w_upsample, bias_upsample, w_conv_first, bias_first, w_conv_second, bias_second,
):
    near, far = tables()
    operands = (
        latents[0], gain_attn, w_query[0], w_key[0], w_value[0], w_out[0], scale_attn, gain_ffn, w_up[0], w_down[0],
        scale_ffn, jnp.transpose(w_lift, (0, 2, 1)), bias_lift[None], w_upsample, bias_upsample[None], w_conv_first,
        bias_first[None], w_conv_second, bias_second[None], jnp.asarray(near), jnp.asarray(far),
    )
    vmem = pltpu.VMEM
    result = pl.pallas_call(
        kernel,
        out_shape=jax.ShapeDtypeStruct((FRAMES * UPS, C1), BF16),
        in_specs=[pl.BlockSpec(memory_space=pl.ANY)] * len(operands),
        out_specs=pl.BlockSpec(memory_space=pl.ANY),
        scratch_shapes=[
            vmem((7, C0, D), BF16),
            vmem((2, UPS, 2, C0, C1 // 2), BF16),
            vmem((ROWS, D), BF16),
            vmem((4, D, D), BF16),
            vmem((D, FF), BF16),
            vmem((FF, D), BF16),
            vmem((C1, 3 * CH), BF16),
            vmem((CH, C1), BF16),
            vmem((1, D), F32),
            vmem((1, D), F32),
            vmem((1, D), F32),
            vmem((1, D), F32),
            vmem((1, C0), F32),
            vmem((1, C1), F32),
            vmem((1, CH), F32),
            vmem((1, C1), F32),
            vmem((2, ROWS, 128), F32),
            vmem((2, 32, 128), F32),
            vmem((LIVE, D), BF16),
            vmem((ROWS, D), BF16),
            vmem((ROWS, D), BF16),
            vmem((LIVE, D), BF16),
            vmem((LIVE, D), F32),
            vmem((LIVE, D), BF16),
            vmem((LIVE, D), F32),
            vmem((LIVE, 7 * D), BF16),
            vmem((LIVE, 2 * C0), BF16),
            vmem((UPS + 2, LIVE, C1), BF16),
            vmem((4, FRAMES * UPS, 128), F32),
            vmem((FRAMES * UPS, C1), BF16),
            pltpu.SemaphoreType.DMA((112,)),
            pltpu.SemaphoreType.DMA((102,)),
            pltpu.SemaphoreType.DMA((24,)),
            pltpu.SemaphoreType.DMA((4,)),
        ],
        compiler_params=pltpu.CompilerParams(collective_id=0, has_side_effects=True, vmem_limit_bytes=60 * 2**20),
        cost_estimate=pl.CostEstimate(flops=11 * 10**9, bytes_accessed=36 * 10**6, transcendentals=4 * 10**6),
    )(*operands)
    return result[None]


def solution(mesh):
    whole = P()
    placed = [whole] * 19
    placed[0] = P("stream", "tm", None)
    placed[11] = P(None, None, "tm")
    placed[13] = P(None, "tm")
    return jax.shard_map(
        body, mesh=mesh, in_specs=tuple(placed), out_specs=P("stream", "tm", None), check_vma=False
    )
```

time: 277 us -> 99.5 us (0.36)
  waiting for transfers between devices: 160 us -> 0 us
  Pallas kernels: 0 us -> 96.2 us
  matrix products: 45 us -> 0 us
  local copies, waits for them, and re-layouts: 33.1 us -> 3.05 us
  starting transfers between devices: 14.4 us -> 0 us
  between operations: 13.9 us -> 0.01 us
  other arithmetic: 9.67 us -> 0 us
    all_gather x2 -> x0, waiting for transfers between devices: 158 us -> none  [the longest x1 115 us: body(): lax.all_gather(w_upsample, 'tm', axis=1, tiled=True)]
    pallas_call x0 -> x1, Pallas kernels: none -> 96.2 us  [body(): pl.pallas_call(kernel, out_shape=jax.ShapeDtypeStruct((FRAMES * UPS, C1),...]
    dot_general x17 -> x0, matrix products: 45 us -> none  [the longest x1 19.1 us: body(): jnp.dot(active_rows, lax.all_gather(w_upsample, 'tm', axis=1, tiled=True)...]
    dot_general x1 -> x0, local copies, waits for them, and re-layouts: 22.4 us -> none  [body(): jnp.dot(active_rows, lax.all_gather(w_upsample, 'tm', axis=1, tiled=True)...]
    ppermute x4 -> x0, starting transfers between devices: 14.3 us -> none  [passed_along(): return lax.ppermute(block, axis, route)]
    slice x5 -> x0, local copies, waits for them, and re-layouts: 5.56 us -> none  [the longest x1 4.62 us: body(): tap_all[:, 2:, 0]]
    convert_element_type x3 -> x0, other arithmetic: 4.8 us -> none  [the longest x1 4.78 us: body(): upsampled = (bias_upsample + tap_all[:, 2:, 0] + tap_all[:, 1:-1, 1]).res...]
  transfers between devices with their start and end apart: 6 -> 0, of which waited for: 3 -> 0; matrix products, arithmetic and copies ran while one was open for 18% -> 0% of each run, Pallas kernels for 0% -> 0%
where the time goes in v1:
time: 99.5 us; the launch traced here: 99.3 us
  Pallas kernels  96.2 us (97%)
  local copies, waits for them, and re-layouts  3.05 us (3%)
    pallas_call x1, Pallas kernels, body(): pl.pallas_call(kernel, out_shape=jax.ShapeDtypeStruct((FRAMES * UPS, C1),...  96.2 us
    unnamed x1, local copies, waits for them, and re-layouts  3.05 us

profile of v1, /device:TPU:1, one launch (start us, length us, event | category | flops | bytes accessed | tf_op | source)
XLA Modules:
  0.0 99.3 jit_solution(7610788700772351965)
XLA Ops:
  0.0 96.2 %shard_map.199 = bf16[2048,512]{1,0:T(8,128)(2,1)} custom-call(bf16[256,512]{1,0:T(8,128)(2,1)} %bitcast.20, f32[1,512]{1,0:T(1,128)} %ga.1, bf16[512,512]{1,0:T(8,128)(2,1)} %bitcast.16, bf16[512,512]{1,0:T(8,128)(2,1)} %bitcast.17, bf16[512,512]{1,0:T(8,128)(2,1)} %bitcast.18, bf16[512,512]{1,0:T(8,128)(2,1)} %bitcast.19, f32[1,512]{1,0:T(1,128)} %sa.1, ...), custom_call_target="tpu_custom_call" | custom-call | flops 11000000512 | bytes 36000000 | tf_op jit(solution)/shard_map/pallas_call | solution.py:447
  96.2 3.0 %copy.23 = bf16[1,2048,512]{2,1,0:T(8,128)(2,1)} copy(bf16[1,2048,512]{2,1,0:T(8,128)(2,1)} %bitcast.13) | data formatting | bytes 4194304

commit v2 on v1

v2 whole, which is shorter than its diff:
```python
import math

import jax
import jax.numpy as jnp
import numpy as np
from jax import lax
from jax.experimental import pallas as pl
from jax.experimental.pallas import tpu as pltpu
from jax.sharding import PartitionSpec as P

MESH = pl.DeviceIdType.MESH
BF16, F32 = jnp.bfloat16, jnp.float32
WIN, UPS = 250, 8
FRAMES, D, FF, C0, C1, CH = 256, 512, 2048, 1024, 512, 256
HALO = 272
ROWS = HALO + FRAMES
LIVE = 272
LEAD = LIVE - FRAMES


def coords():
    t = lax.axis_index("tm")
    s = lax.axis_index("stream")
    return s % 4, (s // 4) * 2 + t // 16, (t // 2) % 8, t % 2


def device(x, y, z, c):
    return ((y % 2) * 16 + z * 2 + c, (y // 2) * 4 + x)


SPANS = {
    "L": {
        "W": (0, 0, 7), "C": (2, 2, 3), "Ca": (2, 2, 2), "Cb": (4, 4, 1), "M": (0, 5, 2), "Ma": (0, 5, 1),
        "Mb": (1, 6, 1), "O": (5, 0, 2), "Oa": (5, 0, 1), "Ob": (6, 1, 1),
    },
    "U": {
        "W": (0, 0, 1024), "C": (336, 336, 352), "Ca": (336, 336, 176), "Cb": (512, 512, 176), "M": (0, 688, 336),
        "Ma": (0, 688, 176), "Mb": (176, 864, 160), "O": (688, 0, 336), "Oa": (688, 0, 176), "Ob": (864, 176, 160),
    },
}
NEAR = (-1, 1, -2, 2, -3, 3)


def routes():
    sends, joins = {}, {}
    for kind in "LU":

        def add(part, row, d, *items):
            got = sends.setdefault((kind, part, row, d), [])
            for name, to_row, to_d, sent, link in items:
                got.append(((kind, name, to_row, to_d), sent, link))

        for q in "MC":
            add("W", 0, 0, (q, 0, -1, q, "z+"), (q, 0, 1, q, "z-"))
        add("W", 0, 0, ("M", 1, 0, "M", "y+"), ("C", 1, 0, "C", "y-"), ("S", 0, 0, "W", "s"))
        add("M", 1, 0, ("Oa", 1, 0, "Ma", "x+"), ("Ob", 1, 0, "Mb", "x-"))
        joins[kind, 1, 0] = ("M", "C", "Oa", "Ob")
        for d in NEAR:
            up, swap = d < 0, d in (-1, 2, -3)
            for q in "MC":
                if abs(d) < 3:
                    add(q, 0, d, (q, 0, d - 1 if up else d + 1, q, "z+" if up else "z-"))
                elif up == (q == "M"):
                    add(q, 0, d, (q, 0, 4, q, "z+" if up else "z-"))
                add(q, 0, d, (q, 1, d, q, "y+" if swap == (q == "M") else "y-"))
            add("M", 0, d, ("O", 0, d, "M", "x+" if swap else "x-"))
            add("M", 1, d, ("O", 1, d, "M", "x-" if swap else "x+"))
            joins[kind, 0, d] = joins[kind, 1, d] = ("M", "C", "O")
        for h, y, x in (("a", "y+", "x+"), ("b", "y-", "x-")):
            add("M", 0, 4, ("M" + h, 1, 4, "M" + h, y), ("O" + h, 0, 4, "M" + h, x))
            add("C", 0, 4, ("C" + h, 1, 4, "C" + h, y))
            add("M" + h, 1, 4, ("O" + h, 1, 4, "M" + h, x))
        joins[kind, 0, 4] = ("M", "C", "Oa", "Ob")
        joins[kind, 1, 4] = ("Ma", "Mb", "Ca", "Cb", "Oa", "Ob")
    return sends, joins


class Gather:
    def __init__(self, wl, wu, lbuf, ubuf, send_sems, recv_sems):
        self.x, self.y, self.z, self.c = x, y, z, c = coords()
        self.xp = self.x % 2
        self.src = {"L": wl, "U": wu}
        self.buf = {"L": lbuf, "U": ubuf}
        self.send_sems, self.recv_sems = send_sems, recv_sems
        self.sent = []
        self.sends, self.joins = routes()
        arrivals = [to for sends in self.sends.values() for to, _, _ in sends]
        arrivals += [(kind, "S", row, d) for kind, row, d in self.joins]
        self.number = {to: i + 2 for i, to in enumerate(arrivals)}
        self.here = set()
        self.to = {
            "z+": device(x, y, (z + 1) % 8, c),
            "z-": device(x, y, (z + 7) % 8, c),
            "y+": device(x, (y + 1) % 4, z, c),
            "y-": device(x, (y + 3) % 4, z, c),
            "x+": device((x + 1) % 4, y, z, c),
            "x-": device((x + 3) % 4, y, z, c),
            "s": device(x, y, z, 1 - c),
        }
        t, s = lax.axis_index("tm"), lax.axis_index("stream")
        self.after = [((t + k) % 32, s) for k in (1, 2)]
        self.before = [((t + 32 - k) % 32, s) for k in (1, 2)]

    def ref(self, kind, part, row, d, core=None, own=False):
        even, odd, size = SPANS[kind][part]
        start = even if even == odd else even + (odd - even) * self.xp
        if kind == "U" and even != odd:
            start = pl.multiple_of(start, 16)
        if own:
            return self.src[kind].at[pl.ds(start, size)]
        yl, zz = (self.y + row) % 2, (self.z + d + 8) % 8
        core = self.c if core is None else core
        if kind == "U":
            return self.buf[kind].at[yl, zz, core, pl.ds(start, size)]
        first = pl.multiple_of(32 * (yl * 16 + zz * 2 + core), 32)
        return self.buf[kind].at[pl.ds(start, size), pl.ds(first, 32)]

    def start(self, src, dst, target, recv):
        copy = pltpu.make_async_remote_copy(
            src_ref=src,
            dst_ref=dst,
            send_sem=self.send_sems.at[len(self.sent)],
            recv_sem=self.recv_sems.at[recv],
            device_id=target,
            device_id_type=MESH,
        )
        copy.start()
        self.sent.append(copy)

    def wait(self, ref, recv):
        pltpu.make_async_remote_copy(
            src_ref=ref,
            dst_ref=ref,
            send_sem=self.send_sems.at[0],
            recv_sem=self.recv_sems.at[recv],
            device_id=self.to["s"],
            device_id_type=MESH,
        ).wait_recv()

    def event(self, kind, part, row, d):
        own = row == 0 and d == 0
        if part == "S":
            self.wait(self.ref(kind, "W", row, d, core=1 - self.c), self.number[kind, part, row, d])
        elif not own:
            self.wait(self.ref(kind, part, row, d), self.number[kind, part, row, d])
        self.here.add((kind, part, row, d))
        for to, sent, link in self.sends.get((kind, part, row, d), ()):
            self.start(
                self.ref(kind, sent, row, d, own=own), self.ref(kind, sent, row, d), self.to[link], self.number[to]
            )
        parts = self.joins.get((kind, row, d), ())
        if part in parts and all((kind, q, row, d) in self.here for q in parts):
            whole = self.ref(kind, "W", row, d)
            self.start(whole, whole, self.to["s"], self.number[kind, "S", row, d])

    def barrier(self):
        semaphore = pltpu.get_barrier_semaphore()
        targets = list(self.to.values()) + self.before
        for target in targets:
            pl.semaphore_signal(semaphore, inc=1, device_id=target, device_id_type=MESH)
        pl.semaphore_wait(semaphore, len(targets))

    def finish(self):
        for copy in self.sent:
            copy.wait_send()


PLAN = (
    ("L", "S", 0, 0), ("L", "M", 0, 1), ("L", "M", 1, 0), ("L", "C", 1, 0), ("norm",), ("L", "C", 0, 1),
    ("L", "Oa", 1, 0), ("L", "M", 0, -1), ("L", "M", 1, 1), ("L", "O", 0, 1), ("k",), ("L", "M", 0, 2),
    ("L", "Ob", 1, 0), ("L", "S", 0, 1), ("L", "C", 0, -1), ("v",), ("q",), ("L", "O", 0, -1), ("L", "S", 1, 0),
    ("L", "M", 0, -2), ("L", "C", 0, 2), ("L", "C", 1, 1), ("att", 0, 0), ("L", "O", 1, 1), ("att", 0, 1),
    ("L", "S", 0, -1), ("L", "M", 0, 3), ("L", "M", 1, -1), ("L", "C", 0, -2), ("L", "C", 1, -1), ("L", "O", 0, 2),
    ("L", "S", 1, 1), ("att", 0, 2), ("L", "M", 1, 2), ("L", "O", 0, -2), ("L", "M", 0, -3), ("L", "M", 1, -2),
    ("att", 1, 0), ("L", "S", 0, 2), ("L", "C", 0, 3), ("att", 1, 1), ("L", "S", 0, -2), ("L", "O", 0, 3),
    ("att", 1, 2), ("L", "C", 1, 2), ("L", "C", 0, -3), ("U", "W", 0, 0), ("L", "C", 1, -2), ("L", "O", 1, -1),
    ("L", "O", 0, -3), ("L", "S", 0, 3), ("L", "M", 1, 3), ("att", 2, 0), ("L", "M", 0, 4), ("L", "M", 1, -3),
    ("L", "O", 1, 2), ("L", "O", 1, -2), ("L", "C", 0, 4), ("U", "S", 0, 0), ("att", 2, 1), ("L", "S", 1, -1),
    ("L", "C", 1, 3), ("L", "S", 0, -3), ("att", 2, 2), ("L", "S", 1, 2), ("L", "C", 1, -3), ("L", "O", 1, 3),
    ("L", "S", 1, -2), ("L", "Ob", 0, 4), ("att", 3, 0), ("L", "Oa", 0, 4), ("att", 3, 1), ("U", "M", 0, -1),
    ("L", "S", 1, 3), ("L", "O", 1, -3), ("U", "M", 0, 1), ("L", "S", 0, 4), ("att", 3, 2), ("U", "M", 1, 0),
    ("post",), ("L", "S", 1, -3), ("L", "Ma", 1, 4), ("U", "C", 1, 0), ("L", "Mb", 1, 4), ("ff", 0),
    ("L", "Ca", 1, 4), ("ff", 1), ("U", "C", 0, -1), ("L", "Cb", 1, 4), ("U", "C", 0, 1), ("ff", 2), ("ff", 3),
    ("ff", 4), ("ff", 5), ("U", "O", 0, -1), ("U", "O", 0, 1), ("ff", 6), ("ff", 7), ("U", "M", 1, -1), ("end",),
    ("U", "M", 0, -2), ("U", "M", 1, 1), ("U", "Oa", 1, 0), ("U", "M", 0, 2), ("U", "Ob", 1, 0), ("U", "S", 0, -1),
    ("L", "Oa", 1, 4), ("L", "Ob", 1, 4), ("U", "S", 0, 1), ("U", "S", 1, 0), ("U", "C", 1, 1), ("L", "S", 1, 4),
    ("la", 0), ("lb", 0), ("U", "C", 0, -2), ("U", "C", 1, -1), ("U", "C", 0, 2), ("la", 1), ("U", "O", 1, -1),
    ("lb", 1), ("la", 2), ("U", "O", 1, 1), ("lb", 2), ("la", 3), ("U", "M", 1, 2), ("U", "S", 1, -1), ("lb", 3),
    ("U", "M", 0, -3), ("U", "M", 1, -2), ("U", "M", 0, 3), ("U", "S", 1, 1), ("up", 0, 0), ("up", 0, 1),
    ("U", "O", 0, -2), ("up", -1, 0), ("up", -1, 1), ("U", "O", 0, 2), ("up", 1, 0), ("up", 1, 1), ("ru", 1),
    ("U", "C", 1, -2), ("U", "S", 0, -2), ("U", "C", 0, -3), ("U", "C", 1, 2), ("U", "C", 0, 3), ("U", "S", 0, 2),
    ("U", "O", 1, 2), ("U", "O", 0, -3), ("U", "S", 1, 2), ("U", "M", 1, -3), ("U", "M", 0, 4), ("U", "M", 1, 3),
    ("U", "S", 0, -3), ("U", "O", 0, 3), ("U", "O", 1, -2), ("U", "C", 0, 4), ("U", "S", 0, 3), ("U", "C", 1, 3),
    ("U", "Oa", 0, 4), ("U", "S", 1, -2), ("up", -2, 0), ("U", "C", 1, -3), ("up", -2, 1), ("U", "O", 1, -3),
    ("ru", 0), ("U", "Ma", 1, 4), ("up", 2, 0), ("U", "Mb", 1, 4), ("up", 2, 1), ("ru", 2), ("U", "Ob", 0, 4),
    ("U", "S", 1, -3), ("U", "Ca", 1, 4), ("up", -3, 0), ("U", "O", 1, 3), ("up", -3, 1), ("U", "Cb", 1, 4),
    ("ru", -1), ("U", "S", 0, 4), ("U", "Oa", 1, 4), ("U", "Ob", 1, 4), ("U", "S", 1, 3), ("up", 3, 0), ("up", 3, 1),
    ("ru", 3), ("U", "S", 1, 4), ("up", 4, 0), ("up", 4, 1), ("ru", 4), ("ru", -2), ("ru", -3),
)


def dot(a, b):
    return jnp.dot(a, b, preferred_element_type=F32)


def dot_nt(a, b):
    return lax.dot_general(a, b, (((1,), (1,)), ((), ())), preferred_element_type=F32)


def elu(v):
    return jnp.where(v > 0, v, jnp.exp(jnp.minimum(v, 0.0)) - 1.0)


def layer_norm(v, gain):
    centred = v - jnp.mean(v, axis=-1, keepdims=True)
    variance = jnp.mean(centred * centred, axis=-1, keepdims=True)
    return centred * lax.rsqrt(variance + 1e-05) * gain


def kernel(
    lat, ga, wq, wk, wv, wo, sa, gf, wup, wdn, sf, wl, bl, wu, bu, wc1, b1, wc2, b2, near, far,
    out,
    lbuf, ubuf, xin, vproj, vup, vdn, vc1, vc2, vga, vsa, vgf, vsf, vbl, vbu, vb1, vb2, vnear, vfar,
    normed, turn, qs, ks, vs, mixed, res, acc, cur7, act2, rect, ups, obf,
    send_sems, recv_sems, here_sems, out_sems,
):
    g = Gather(wl, wu, lbuf, ubuf, send_sems, recv_sems)
    t = lax.axis_index("tm")
    here = []

    def bring(src, dst):
        copy = pltpu.make_async_copy(src, dst, here_sems.at[len(here)])
        copy.start()
        here.append(copy)
        return copy

    own_x = bring(lat, xin.at[pl.ds(HALO, FRAMES)])
    in_ga, in_near, in_far = bring(ga, vga), bring(near, vnear), bring(far, vfar)
    g.barrier()
    g.start(lat, xin.at[pl.ds(LEAD, FRAMES)], g.after[0], 0)
    g.start(lat.at[pl.ds(FRAMES - LEAD, LEAD)], xin.at[pl.ds(0, LEAD)], g.after[1], 1)
    g.event("L", "W", 0, 0)
    in_proj = [bring(w, vproj.at[i]) for i, w in enumerate((wk, wv, wq, wo))]
    own_l = bring(wl, g.ref("L", "W", 0, 0))
    own_u = bring(wu, g.ref("U", "W", 0, 0))
    in_up, in_dn = bring(wup, vup), bring(wdn, vdn)
    in_vec = [
        bring(a, b)
        for a, b in ((sa, vsa), (gf, vgf), (sf, vsf), (bl, vbl), (bu, vbu), (b1, vb1), (b2, vb2))
    ]
    in_c1, in_c2 = bring(wc1, vc1), bring(wc2, vc2)

    lane = lax.broadcasted_iota(jnp.int32, (1, 128), 1)
    first, low = lane % 64 < 32, lane < 64
    live_row = lax.broadcasted_iota(jnp.int32, (LIVE, 1), 0)
    real = (live_row >= LEAD) | (t > 0)
    tail = ROWS - LIVE

    def first_norm():
        own_x.wait()
        g.wait(xin.at[pl.ds(LEAD, FRAMES)], 0)
        g.wait(xin.at[pl.ds(0, LEAD)], 1)
        for copy in (in_ga, in_near, in_far):
            copy.wait()
        normed[...] = layer_norm(xin[...].astype(F32), vga[...]).astype(BF16)
        cos_a, sin_a = vfar[0, pl.ds(t, 1), :], vfar[1, pl.ds(t, 1), :]
        cos_b, sin_b = vnear[0], vnear[1]
        turn[0] = cos_a * cos_b - sin_a * sin_b
        sine = sin_a * cos_b + cos_a * sin_b
        turn[1] = jnp.where(first, -sine, sine)

    def rope(v, skip):
        parts = []
        for i in range(4):
            block = v[:, 128 * i : 128 * i + 128]
            other = jnp.where(first, pltpu.roll(block, 96, 1), pltpu.roll(block, 32, 1))
            parts.append(block * turn[0, skip:] + other * turn[1, skip:])
        return jnp.concatenate(parts, axis=1).astype(BF16)

    def keys():
        in_proj[0].wait()
        ks[...] = rope(dot(normed[...], vproj[0]), 0)

    def values():
        in_proj[1].wait()
        vs[...] = dot(normed[...], vproj[1]).astype(BF16)

    def queries():
        in_proj[2].wait()
        qs[...] = rope(dot(normed[tail:], vproj[2]), tail) * BF16(0.125)

    def attention(pair, block):
        lanes = slice(128 * pair, 128 * pair + 128)
        q0, size, k0, width = ((256, 96, 0, 352), (352, 96, 96, 352), (448, 80, 192, 336))[block]
        q_row = q0 + lax.broadcasted_iota(jnp.int32, (size, width), 0)
        k_row = k0 + lax.broadcasted_iota(jnp.int32, (size, width), 1)
        allowed = (k_row <= q_row) & (k_row > q_row - WIN) & (k_row >= HALO - FRAMES * t)
        q = qs[q0 - tail : q0 - tail + size, lanes]
        k, v = ks[k0 : k0 + width, lanes], vs[k0 : k0 + width, lanes]
        halves = []
        for mask in (low, ~low):
            scores = jnp.where(allowed, dot_nt(jnp.where(mask, q, BF16(0)), k), -1e30)
            weights = jnp.exp(scores - jnp.max(scores, axis=-1, keepdims=True))
            weights = jnp.where(allowed, weights, 0.0)
            total = jnp.maximum(jnp.sum(weights, axis=-1, keepdims=True), 0.5)
            halves.append(dot((weights / total).astype(BF16), v))
        mixed[q0 - tail : q0 - tail + size, lanes] = jnp.where(low, *halves).astype(BF16)

    def after_attention():
        in_proj[3].wait()
        for copy in in_vec:
            copy.wait()
        state = xin[tail:, :].astype(F32)
        residual = state + vsa[...] * dot(mixed[...], vproj[3])
        res[...] = residual
        normed[:LIVE] = layer_norm(residual, vgf[...]).astype(BF16)
        in_up.wait()
        in_dn.wait()

    def feed_forward(i):
        cols = slice(256 * i, 256 * i + 256)
        v = dot(normed[:LIVE], vup[:, cols])
        hidden = (0.5 * v * (1.0 + lax.erf(v * (1.0 / math.sqrt(2.0))))).astype(BF16)
        part = dot(hidden, vdn[cols, :])
        acc[...] = part if i == 0 else acc[...] + part

    def layer_end():
        current = (res[...] + vsf[...] * acc[...]).astype(BF16).astype(F32)
        current = jnp.where(real, current, 0.0)
        for m in range(7):
            moved = pltpu.roll(current, 6 - m, 0) if m < 6 else current
            cur7[:, 512 * m : 512 * m + 512] = moved.astype(BF16)

    def taps(rows, which):
        return sum(dot_nt(cur7[:, 512 * m : 512 * m + 512], lbuf[m, rows, :]) for m in which)

    def lift_begin(i):
        if i == 0:
            own_l.wait()
        acc[:, :256] = taps(slice(256 * i, 256 * i + 256), range(4)) + vbl[:, 256 * i : 256 * i + 256]

    def lift_end(i):
        cols = slice(256 * i, 256 * i + 256)
        total = acc[:, :256] + taps(cols, range(4, 7))
        active = jnp.where(real, elu(total), 0.0).astype(BF16)
        act2[:, cols] = active
        act2[:, C0 + 256 * i : C0 + 256 * i + 256] = pltpu.roll(active.astype(F32), 1, 0).astype(BF16)

    def upsample(d, half):
        if (d, half) == (0, 0):
            own_u.wait()
            in_c1.wait()
            in_c2.wait()
        j = (g.z + d + 8) % 8
        cols = slice(256 * half, 256 * half + 256)
        up = dot(act2[:, :C0], ubuf[0, j, half]) + dot(act2[:, C0:], ubuf[1, j, half])
        up = (up + vbu[:, cols]).astype(BF16)
        ups[j, :, cols] = up[LEAD:]
        rectified = jnp.where(real, elu(up.astype(F32)), 0.0)
        rect[j + 2, :, cols] = rectified.astype(BF16)

        @pl.when(j >= 6)
        def _():
            rect[j - 6, :, cols] = pltpu.roll(rectified, 1, 0).astype(BF16)

    leaving = []

    def residual_unit(d):
        j = (g.z + d + 8) % 8
        total = vb1[...]
        for m in range(3):
            total = total + dot(rect[j + m, LEAD:], vc1[:, CH * m : CH * m + CH])
        second = dot(elu(total).astype(BF16), vc2[...])
        obf[j] = (ups[j].astype(F32) + vb2[...] + second).astype(BF16)
        copy = pltpu.make_async_copy(obf.at[j], out.at[j], out_sems.at[len(leaving)])
        copy.start()
        leaving.append(copy)

    steps = dict(
        norm=first_norm, k=keys, v=values, q=queries, att=attention, post=after_attention, ff=feed_forward,
        end=layer_end, la=lift_begin, lb=lift_end, up=upsample, ru=residual_unit,
    )
    for name, *where in PLAN:
        if name in steps:
            steps[name](*where)
        else:
            g.event(name, *where)
    for copy in leaving:
        copy.wait()
    g.finish()


def weave(phases, out, rows):
    for i in range(4):
        lanes = slice(128 * i, 128 * i + 128)
        for j in range(UPS):
            rows[i, pl.ds(j, phases.shape[1], stride=UPS), :] = phases[j, :, lanes].astype(F32)
        out[:, lanes] = rows[i].astype(BF16)


def tables():
    frequency = 10000.0 ** (-np.arange(32, dtype=np.float64) / 32)
    frequency = np.tile(frequency, 4)[None, :]

    def both(frames):
        angles = frames[:, None] * frequency
        return np.stack([np.cos(angles), np.sin(angles)]).astype(np.float32)

    return both(np.arange(ROWS) - float(HALO)), both(np.arange(32) * float(FRAMES))


def body(
    latents, gain_attn, w_query, w_key, w_value, w_out, scale_attn, gain_ffn, w_up, w_down, scale_ffn,
    w_lift, bias_lift, w_upsample, bias_upsample, w_conv_first, bias_first, w_conv_second, bias_second,
):
    near, far = tables()
    operands = (
        latents[0], gain_attn, w_query[0], w_key[0], w_value[0], w_out[0], scale_attn, gain_ffn, w_up[0], w_down[0],
        scale_ffn, jnp.transpose(w_lift, (0, 2, 1)), bias_lift[None], w_upsample, bias_upsample[None], w_conv_first,
        bias_first[None], w_conv_second, bias_second[None], jnp.asarray(near), jnp.asarray(far),
    )
    vmem = pltpu.VMEM
    dma = pltpu.SemaphoreType.DMA
    phases = pl.pallas_call(
        kernel,
        out_shape=jax.ShapeDtypeStruct((UPS, FRAMES, C1), BF16),
        in_specs=[pl.BlockSpec(memory_space=pl.ANY)] * len(operands),
        out_specs=pl.BlockSpec(memory_space=pl.ANY),
        scratch_shapes=[
            vmem((7, C0, D), BF16),
            vmem((2, UPS, 2, C0, C1 // 2), BF16),
            vmem((ROWS, D), BF16),
            vmem((4, D, D), BF16),
            vmem((D, FF), BF16),
            vmem((FF, D), BF16),
            vmem((C1, 3 * CH), BF16),
            vmem((CH, C1), BF16),
            vmem((1, D), F32),
            vmem((1, D), F32),
            vmem((1, D), F32),
            vmem((1, D), F32),
            vmem((1, C0), F32),
            vmem((1, C1), F32),
            vmem((1, CH), F32),
            vmem((1, C1), F32),
            vmem((2, ROWS, 128), F32),
            vmem((2, 32, 128), F32),
            vmem((ROWS, D), BF16),
            vmem((2, ROWS, 128), F32),
            vmem((LIVE, D), BF16),
            vmem((ROWS, D), BF16),
            vmem((ROWS, D), BF16),
            vmem((LIVE, D), BF16),
            vmem((LIVE, D), F32),
            vmem((LIVE, D), F32),
            vmem((LIVE, 7 * D), BF16),
            vmem((LIVE, 2 * C0), BF16),
            vmem((UPS + 2, LIVE, C1), BF16),
            vmem((UPS, FRAMES, C1), BF16),
            vmem((UPS, FRAMES, C1), BF16),
            dma((140,)),
            dma((140,)),
            dma((24,)),
            dma((8,)),
        ],
        compiler_params=pltpu.CompilerParams(collective_id=0, has_side_effects=True, vmem_limit_bytes=60 * 2**20),
        cost_estimate=pl.CostEstimate(flops=11 * 10**9, bytes_accessed=36 * 10**6, transcendentals=4 * 10**6),
    )(*operands)
    block = 64
    result = pl.pallas_call(
        weave,
        out_shape=jax.ShapeDtypeStruct((FRAMES * UPS, C1), BF16),
        grid=(FRAMES // block,),
        in_specs=[pl.BlockSpec((UPS, block, C1), lambda i: (0, i, 0))],
        out_specs=pl.BlockSpec((UPS * block, C1), lambda i: (i, 0)),
        scratch_shapes=[vmem((4, UPS * block, 128), F32)],
    )(phases)
    return result[None]


def solution(mesh):
    whole = P()
    placed = [whole] * 19
    placed[0] = P("stream", "tm", None)
    placed[11] = P(None, None, "tm")
    placed[13] = P(None, "tm")
    return jax.shard_map(
        body, mesh=mesh, in_specs=tuple(placed), out_specs=P("stream", "tm", None), check_vma=False
    )
```

time: 99.5 us -> 84.9 us (0.85)
  Pallas kernels: 96.2 us -> 84.8 us
  local copies, waits for them, and re-layouts: 3.05 us -> 0 us
    pallas_call x1 -> x2, Pallas kernels: 96.2 us -> 84.8 us  [the longest x1 80.4 us: body(): pl.pallas_call(kernel, out_shape=jax.ShapeDtypeStruct((UPS, FRAMES, C1),...]
    unnamed x1 -> x0, local copies, waits for them, and re-layouts: 3.05 us -> none
where the time goes in v2:
time: 84.9 us; the launch traced here: 84.8 us
  Pallas kernels  84.8 us (100%)
    pallas_call x1, Pallas kernels, body(): pl.pallas_call(kernel, out_shape=jax.ShapeDtypeStruct((UPS, FRAMES, C1),...  80.4 us
    pallas_call x1, Pallas kernels, body(): pl.pallas_call(weave, out_shape=jax.ShapeDtypeStruct((FRAMES * UPS, C1),...  4.34 us

profile of v2, /device:TPU:1, one launch (start us, length us, event | category | flops | bytes accessed | tf_op | source)
XLA Modules:
  0.0 84.8 jit_solution(3061975301442813061)
XLA Ops:
  0.0 80.4 %shard_map.199.phases = bf16[8,256,512]{2,1,0:T(8,128)(2,1)} custom-call(bf16[256,512]{1,0:T(8,128)(2,1)} %bitcast.19, f32[1,512]{1,0:T(1,128)} %ga.1, bf16[512,512]{1,0:T(8,128)(2,1)} %bitcast.15, bf16[512,512]{1,0:T(8,128)(2,1)} %bitcast.16, bf16[512,512]{1,0:T(8,128)(2,1)} %bitcast.17, bf16[512,512]{1,0:T(8,128)(2,1)} %bitcast.18, f32[1,512]{1,0:T(1,128)} %sa.1, ...), custom_call_target="tpu_custom_call" | custom-call | flops 11000000512 | bytes 36000000 | tf_op jit(solution)/shard_map/pallas_call | solution.py:424
  80.4 4.3 %shard_map.200 = bf16[2048,512]{1,0:T(8,128)(2,1)} custom-call(bf16[8,256,512]{2,1,0:T(8,128)(2,1)} %shard_map.199.phases), custom_call_target="tpu_custom_call" | custom-call | tf_op jit(solution)/shard_map/pallas_call | solution.py:470

commit v3 on v2

--- a/solution.py
+++ b/solution.py
@@ -30,48 +30,60 @@
 
 SPANS = {
     "L": {
-        "W": (0, 0, 7), "C": (2, 2, 3), "Ca": (2, 2, 2), "Cb": (4, 4, 1), "M": (0, 5, 2), "Ma": (0, 5, 1),
-        "Mb": (1, 6, 1), "O": (5, 0, 2), "Oa": (5, 0, 1), "Ob": (6, 1, 1),
+        "W": (0, 0, 7), "P": (0, 2, 5), "C": (2, 2, 3), "Ca": (2, 2, 2), "Cb": (4, 4, 1), "M": (0, 5, 2),
+        "Ma": (0, 5, 1), "Mb": (1, 6, 1), "O": (5, 0, 2), "Oa": (5, 0, 1), "Ob": (6, 1, 1),
     },
     "U": {
-        "W": (0, 0, 1024), "C": (336, 336, 352), "Ca": (336, 336, 176), "Cb": (512, 512, 176), "M": (0, 688, 336),
-        "Ma": (0, 688, 176), "Mb": (176, 864, 160), "O": (688, 0, 336), "Oa": (688, 0, 176), "Ob": (864, 176, 160),
+        "W": (0, 0, 1024), "P": (0, 336, 688), "C": (336, 336, 352), "Ca": (336, 336, 176), "Cb": (512, 512, 176),
+        "M": (0, 688, 336), "Ma": (0, 688, 176), "Mb": (176, 864, 160), "O": (688, 0, 336), "Oa": (688, 0, 176),
+        "Ob": (864, 176, 160),
     },
 }
+FROM_CORE = {"S": "W", "SP": "P", "SO": "O"}
 NEAR = (-1, 1, -2, 2, -3, 3)
+SPLIT_CORE = {"L": False, "U": True}
 
 
 def routes():
-    sends, joins = {}, {}
+    sends, joins = {}, []
     for kind in "LU":
+        split = SPLIT_CORE[kind]
 
         def add(part, row, d, *items):
             got = sends.setdefault((kind, part, row, d), [])
             for name, to_row, to_d, sent, link in items:
                 got.append(((kind, name, to_row, to_d), sent, link))
 
-        for q in "MC":
-            add("W", 0, 0, (q, 0, -1, q, "z+"), (q, 0, 1, q, "z-"))
-        add("W", 0, 0, ("M", 1, 0, "M", "y+"), ("C", 1, 0, "C", "y-"), ("S", 0, 0, "W", "s"))
+        def join(row, d, p_parts, o_parts):
+            if split:
+                joins.append((kind, row, d, p_parts, "SP"))
+                joins.append((kind, row, d, o_parts, "SO"))
+            else:
+                joins.append((kind, row, d, p_parts + o_parts, "S"))
+
+        for p in "MC":
+            add(p, 0, 0, (p, 0, -1, p, "z+"), (p, 0, 1, p, "z-"), (p, 1, 0, p, "y+" if p == "M" else "y-"))
+        add("C", 0, 0, ("S", 0, 0, "W", "s"))
         add("M", 1, 0, ("Oa", 1, 0, "Ma", "x+"), ("Ob", 1, 0, "Mb", "x-"))
-        joins[kind, 1, 0] = ("M", "C", "Oa", "Ob")
+        join(1, 0, ("M", "C"), ("Oa", "Ob"))
         for d in NEAR:
             up, swap = d < 0, d in (-1, 2, -3)
-            for q in "MC":
+            for p in "MC":
                 if abs(d) < 3:
-                    add(q, 0, d, (q, 0, d - 1 if up else d + 1, q, "z+" if up else "z-"))
-                elif up == (q == "M"):
-                    add(q, 0, d, (q, 0, 4, q, "z+" if up else "z-"))
-                add(q, 0, d, (q, 1, d, q, "y+" if swap == (q == "M") else "y-"))
-            add("M", 0, d, ("O", 0, d, "M", "x+" if swap else "x-"))
-            add("M", 1, d, ("O", 1, d, "M", "x-" if swap else "x+"))
-            joins[kind, 0, d] = joins[kind, 1, d] = ("M", "C", "O")
-        for h, y, x in (("a", "y+", "x+"), ("b", "y-", "x-")):
-            add("M", 0, 4, ("M" + h, 1, 4, "M" + h, y), ("O" + h, 0, 4, "M" + h, x))
-            add("C", 0, 4, ("C" + h, 1, 4, "C" + h, y))
-            add("M" + h, 1, 4, ("O" + h, 1, 4, "M" + h, x))
-        joins[kind, 0, 4] = ("M", "C", "Oa", "Ob")
-        joins[kind, 1, 4] = ("Ma", "Mb", "Ca", "Cb", "Oa", "Ob")
+                    add(p, 0, d, (p, 0, d - 1 if up else d + 1, p, "z+" if up else "z-"))
+                else:
+                    half = p + ("a" if up else "b")
+                    add(p, 0, d, (half, 0, 4, half, "z+" if up else "z-"))
+                add(p, 0, d, (p, 1, d, p, "y+" if swap == (p == "M") else "y-"))
+            for row in (0, 1):
+                add("M", row, d, ("O", row, d, "M", "x+" if swap == (row == 0) else "x-"))
+                join(row, d, ("M", "C"), ("O",))
+        for p, y in (("Ma", "y+"), ("Mb", "y-"), ("Ca", "y+"), ("Cb", "y-")):
+            add(p, 0, 4, (p, 1, 4, p, y))
+        for row in (0, 1):
+            add("Ma", row, 4, ("Oa", row, 4, "Ma", "x+"))
+            add("Mb", row, 4, ("Ob", row, 4, "Mb", "x-"))
+            join(row, 4, ("Ma", "Mb", "Ca", "Cb"), ("Oa", "Ob"))
     return sends, joins
 
 
@@ -85,7 +97,7 @@
         self.sent = []
         self.sends, self.joins = routes()
         arrivals = [to for sends in self.sends.values() for to, _, _ in sends]
-        arrivals += [(kind, "S", row, d) for kind, row, d in self.joins]
+        arrivals += [(kind, name, row, d) for kind, row, d, _, name in self.joins]
         self.number = {to: i + 2 for i, to in enumerate(arrivals)}
         self.here = set()
         self.to = {
@@ -139,8 +151,8 @@
 
     def event(self, kind, part, row, d):
         own = row == 0 and d == 0
-        if part == "S":
-            self.wait(self.ref(kind, "W", row, d, core=1 - self.c), self.number[kind, part, row, d])
+        if part in FROM_CORE:
+            self.wait(self.ref(kind, FROM_CORE[part], row, d, core=1 - self.c), self.number[kind, part, row, d])
         elif not own:
             self.wait(self.ref(kind, part, row, d), self.number[kind, part, row, d])
         self.here.add((kind, part, row, d))
@@ -148,10 +160,11 @@
             self.start(
                 self.ref(kind, sent, row, d, own=own), self.ref(kind, sent, row, d), self.to[link], self.number[to]
             )
-        parts = self.joins.get((kind, row, d), ())
-        if part in parts and all((kind, q, row, d) in self.here for q in parts):
-            whole = self.ref(kind, "W", row, d)
-            self.start(whole, whole, self.to["s"], self.number[kind, "S", row, d])
+        for of_kind, of_row, of_d, parts, name in self.joins:
+            if (of_kind, of_row, of_d) == (kind, row, d) and part in parts:
+                if all((kind, p, row, d) in self.here for p in parts):
+                    whole = self.ref(kind, FROM_CORE[name], row, d)
+                    self.start(whole, whole, self.to["s"], self.number[kind, name, row, d])
 
     def barrier(self):
         semaphore = pltpu.get_barrier_semaphore()
@@ -167,35 +180,37 @@
 
 PLAN = (
     ("L", "S", 0, 0), ("L", "M", 0, 1), ("L", "M", 1, 0), ("L", "C", 1, 0), ("norm",), ("L", "C", 0, 1),
-    ("L", "Oa", 1, 0), ("L", "M", 0, -1), ("L", "M", 1, 1), ("L", "O", 0, 1), ("k",), ("L", "M", 0, 2),
-    ("L", "Ob", 1, 0), ("L", "S", 0, 1), ("L", "C", 0, -1), ("v",), ("q",), ("L", "O", 0, -1), ("L", "S", 1, 0),
-    ("L", "M", 0, -2), ("L", "C", 0, 2), ("L", "C", 1, 1), ("att", 0, 0), ("L", "O", 1, 1), ("att", 0, 1),
-    ("L", "S", 0, -1), ("L", "M", 0, 3), ("L", "M", 1, -1), ("L", "C", 0, -2), ("L", "C", 1, -1), ("L", "O", 0, 2),
-    ("L", "S", 1, 1), ("att", 0, 2), ("L", "M", 1, 2), ("L", "O", 0, -2), ("L", "M", 0, -3), ("L", "M", 1, -2),
-    ("att", 1, 0), ("L", "S", 0, 2), ("L", "C", 0, 3), ("att", 1, 1), ("L", "S", 0, -2), ("L", "O", 0, 3),
-    ("att", 1, 2), ("L", "C", 1, 2), ("L", "C", 0, -3), ("U", "W", 0, 0), ("L", "C", 1, -2), ("L", "O", 1, -1),
-    ("L", "O", 0, -3), ("L", "S", 0, 3), ("L", "M", 1, 3), ("att", 2, 0), ("L", "M", 0, 4), ("L", "M", 1, -3),
-    ("L", "O", 1, 2), ("L", "O", 1, -2), ("L", "C", 0, 4), ("U", "S", 0, 0), ("att", 2, 1), ("L", "S", 1, -1),
-    ("L", "C", 1, 3), ("L", "S", 0, -3), ("att", 2, 2), ("L", "S", 1, 2), ("L", "C", 1, -3), ("L", "O", 1, 3),
-    ("L", "S", 1, -2), ("L", "Ob", 0, 4), ("att", 3, 0), ("L", "Oa", 0, 4), ("att", 3, 1), ("U", "M", 0, -1),
-    ("L", "S", 1, 3), ("L", "O", 1, -3), ("U", "M", 0, 1), ("L", "S", 0, 4), ("att", 3, 2), ("U", "M", 1, 0),
-    ("post",), ("L", "S", 1, -3), ("L", "Ma", 1, 4), ("U", "C", 1, 0), ("L", "Mb", 1, 4), ("ff", 0),
-    ("L", "Ca", 1, 4), ("ff", 1), ("U", "C", 0, -1), ("L", "Cb", 1, 4), ("U", "C", 0, 1), ("ff", 2), ("ff", 3),
-    ("ff", 4), ("ff", 5), ("U", "O", 0, -1), ("U", "O", 0, 1), ("ff", 6), ("ff", 7), ("U", "M", 1, -1), ("end",),
-    ("U", "M", 0, -2), ("U", "M", 1, 1), ("U", "Oa", 1, 0), ("U", "M", 0, 2), ("U", "Ob", 1, 0), ("U", "S", 0, -1),
-    ("L", "Oa", 1, 4), ("L", "Ob", 1, 4), ("U", "S", 0, 1), ("U", "S", 1, 0), ("U", "C", 1, 1), ("L", "S", 1, 4),
-    ("la", 0), ("lb", 0), ("U", "C", 0, -2), ("U", "C", 1, -1), ("U", "C", 0, 2), ("la", 1), ("U", "O", 1, -1),
-    ("lb", 1), ("la", 2), ("U", "O", 1, 1), ("lb", 2), ("la", 3), ("U", "M", 1, 2), ("U", "S", 1, -1), ("lb", 3),
-    ("U", "M", 0, -3), ("U", "M", 1, -2), ("U", "M", 0, 3), ("U", "S", 1, 1), ("up", 0, 0), ("up", 0, 1),
-    ("U", "O", 0, -2), ("up", -1, 0), ("up", -1, 1), ("U", "O", 0, 2), ("up", 1, 0), ("up", 1, 1), ("ru", 1),
-    ("U", "C", 1, -2), ("U", "S", 0, -2), ("U", "C", 0, -3), ("U", "C", 1, 2), ("U", "C", 0, 3), ("U", "S", 0, 2),
-    ("U", "O", 1, 2), ("U", "O", 0, -3), ("U", "S", 1, 2), ("U", "M", 1, -3), ("U", "M", 0, 4), ("U", "M", 1, 3),
-    ("U", "S", 0, -3), ("U", "O", 0, 3), ("U", "O", 1, -2), ("U", "C", 0, 4), ("U", "S", 0, 3), ("U", "C", 1, 3),
-    ("U", "Oa", 0, 4), ("U", "S", 1, -2), ("up", -2, 0), ("U", "C", 1, -3), ("up", -2, 1), ("U", "O", 1, -3),
-    ("ru", 0), ("U", "Ma", 1, 4), ("up", 2, 0), ("U", "Mb", 1, 4), ("up", 2, 1), ("ru", 2), ("U", "Ob", 0, 4),
-    ("U", "S", 1, -3), ("U", "Ca", 1, 4), ("up", -3, 0), ("U", "O", 1, 3), ("up", -3, 1), ("U", "Cb", 1, 4),
-    ("ru", -1), ("U", "S", 0, 4), ("U", "Oa", 1, 4), ("U", "Ob", 1, 4), ("U", "S", 1, 3), ("up", 3, 0), ("up", 3, 1),
-    ("ru", 3), ("U", "S", 1, 4), ("up", 4, 0), ("up", 4, 1), ("ru", 4), ("ru", -2), ("ru", -3),
+    ("L", "M", 0, -1), ("k",), ("L", "Oa", 1, 0), ("L", "M", 0, 2), ("L", "M", 1, 1), ("L", "O", 0, 1), ("v",),
+    ("L", "Ob", 1, 0), ("L", "C", 0, -1), ("U", "M", 0, 0), ("q",), ("L", "S", 0, 1), ("att", 0, 0), ("L", "S", 1, 0),
+    ("L", "M", 0, -2), ("L", "O", 0, -1), ("att", 0, 1), ("L", "C", 0, 2), ("L", "C", 1, 1), ("att", 0, 2),
+    ("L", "O", 0, 2), ("L", "S", 0, -1), ("L", "M", 0, 3), ("L", "M", 1, -1), ("att", 1, 0), ("L", "O", 1, 1),
+    ("L", "C", 0, -2), ("L", "C", 1, -1), ("att", 1, 1), ("L", "M", 1, 2), ("L", "S", 0, 2), ("L", "O", 0, -2),
+    ("att", 1, 2), ("L", "M", 1, -2), ("L", "S", 1, 1), ("att", 2, 0), ("L", "S", 0, -2), ("U", "M", 0, 1),
+    ("L", "O", 0, 3), ("att", 2, 1), ("L", "C", 1, 2), ("U", "M", 0, -1), ("att", 2, 2), ("U", "M", 1, 0),
+    ("L", "O", 1, -1), ("L", "C", 0, 3), ("L", "M", 1, 3), ("L", "M", 0, -3), ("att", 3, 0), ("L", "Mb", 0, 4),
+    ("L", "O", 1, 2), ("L", "O", 1, -2), ("L", "C", 1, -2), ("U", "C", 0, 0), ("L", "S", 1, -1), ("att", 3, 1),
+    ("L", "S", 0, 3), ("L", "C", 0, -3), ("att", 3, 2), ("L", "S", 1, 2), ("L", "S", 1, -2), ("post",),
+    ("U", "S", 0, 0), ("U", "M", 1, 1), ("U", "M", 0, 2), ("ff", 0), ("U", "O", 0, 1), ("L", "Mb", 1, 4),
+    ("L", "Cb", 0, 4), ("U", "M", 1, -1), ("U", "O", 0, -1), ("ff", 1), ("ff", 2), ("U", "M", 0, -2),
+    ("U", "SO", 0, 1), ("U", "Ob", 1, 0), ("ff", 3), ("U", "SO", 0, -1), ("L", "Ma", 0, 4), ("L", "Ob", 0, 4),
+    ("U", "Oa", 1, 0), ("ff", 4), ("L", "C", 1, 3), ("ff", 5), ("ff", 6), ("L", "Ob", 1, 4), ("U", "SO", 1, 0),
+    ("L", "O", 1, 3), ("L", "M", 1, -3), ("U", "C", 1, 0), ("U", "C", 0, 1), ("ff", 7), ("end",), ("L", "O", 0, -3),
+    ("L", "S", 1, 3), ("U", "C", 0, -1), ("U", "SP", 1, 0), ("L", "C", 1, -3), ("U", "SP", 0, 1), ("L", "Cb", 1, 4),
+    ("L", "S", 0, -3), ("L", "Ca", 0, 4), ("U", "O", 1, -1), ("U", "M", 1, 2), ("U", "SP", 0, -1), ("U", "M", 0, 3),
+    ("L", "Ma", 1, 4), ("U", "SO", 1, -1), ("U", "O", 1, 1), ("U", "SO", 1, 1), ("U", "M", 1, -2), ("U", "M", 0, -3),
+    ("U", "O", 0, -2), ("U", "C", 0, 2), ("U", "C", 1, 1), ("U", "SO", 0, -2), ("L", "O", 1, -3), ("U", "O", 0, 2),
+    ("U", "SP", 0, 2), ("L", "Oa", 0, 4), ("U", "Mb", 0, 4), ("L", "Ca", 1, 4), ("U", "SP", 1, 1), ("L", "Oa", 1, 4),
+    ("L", "S", 1, -3), ("U", "C", 1, -1), ("U", "SO", 0, 2), ("U", "C", 0, -2), ("L", "S", 0, 4), ("L", "S", 1, 4),
+    ("lift", 0), ("U", "O", 1, 2), ("U", "SP", 1, -1), ("lift", 1), ("U", "Ma", 0, 4), ("U", "SP", 0, -2),
+    ("lift", 2), ("U", "M", 1, -3), ("U", "SO", 1, 2), ("U", "O", 1, -2), ("U", "C", 0, 3), ("U", "M", 1, 3),
+    ("lift", 3), ("up", 0, ()), ("U", "SO", 1, -2), ("U", "O", 0, 3), ("U", "SP", 0, 3), ("up", -1, ()),
+    ("U", "C", 0, -3), ("U", "C", 1, -2), ("U", "SO", 0, 3), ("U", "O", 0, -3), ("U", "Ob", 0, 4), ("up", 1, ()),
+    ("U", "C", 1, 2), ("U", "Cb", 0, 4), ("U", "SP", 0, -3), ("U", "Ma", 1, 4), ("U", "Oa", 0, 4), ("U", "SP", 1, -2),
+    ("up", -2, (1,)), ("U", "Mb", 1, 4), ("U", "SO", 0, -3), ("U", "SP", 1, 2), ("U", "SO", 0, 4), ("U", "O", 1, -3),
+    ("up", 2, (0,)), ("U", "Ca", 0, 4), ("U", "SO", 1, -3), ("U", "C", 1, 3), ("U", "O", 1, 3), ("U", "C", 1, -3),
+    ("U", "SP", 0, 4), ("U", "Oa", 1, 4), ("U", "SP", 1, 3), ("U", "Ob", 1, 4), ("U", "SO", 1, 3), ("U", "Cb", 1, 4),
+    ("U", "SP", 1, -3), ("up", -3, (2,)), ("U", "SO", 1, 4), ("U", "Ca", 1, 4), ("up", 3, (-1,)), ("U", "SP", 1, 4),
+    ("early", 3), ("row",), ("up", 4, ()), ("last",),
 )
 
 
@@ -221,7 +236,7 @@
     lat, ga, wq, wk, wv, wo, sa, gf, wup, wdn, sf, wl, bl, wu, bu, wc1, b1, wc2, b2, near, far,
     out,
     lbuf, ubuf, xin, vproj, vup, vdn, vc1, vc2, vga, vsa, vgf, vsf, vbl, vbu, vb1, vb2, vnear, vfar,
-    normed, turn, qs, ks, vs, mixed, res, acc, cur7, act2, rect, ups, obf,
+    normed, turn, qs, ks, vs, mixed, res, acc, cur7, act2, rect, part, ups, obf,
     send_sems, recv_sems, here_sems, out_sems,
 ):
     g = Gather(wl, wu, lbuf, ubuf, send_sems, recv_sems)
@@ -239,7 +254,8 @@
     g.barrier()
     g.start(lat, xin.at[pl.ds(LEAD, FRAMES)], g.after[0], 0)
     g.start(lat.at[pl.ds(FRAMES - LEAD, LEAD)], xin.at[pl.ds(0, LEAD)], g.after[1], 1)
-    g.event("L", "W", 0, 0)
+    g.event("L", "M", 0, 0)
+    g.event("L", "C", 0, 0)
     in_proj = [bring(w, vproj.at[i]) for i, w in enumerate((wk, wv, wq, wo))]
     own_l = bring(wl, g.ref("L", "W", 0, 0))
     own_u = bring(wu, g.ref("U", "W", 0, 0))
@@ -321,8 +337,8 @@
         cols = slice(256 * i, 256 * i + 256)
         v = dot(normed[:LIVE], vup[:, cols])
         hidden = (0.5 * v * (1.0 + lax.erf(v * (1.0 / math.sqrt(2.0))))).astype(BF16)
-        part = dot(hidden, vdn[cols, :])
-        acc[...] = part if i == 0 else acc[...] + part
+        more = dot(hidden, vdn[cols, :])
+        acc[...] = more if i == 0 else acc[...] + more
 
     def layer_end():
         current = (res[...] + vsf[...] * acc[...]).astype(BF16).astype(F32)
@@ -331,54 +347,82 @@
             moved = pltpu.roll(current, 6 - m, 0) if m < 6 else current
             cur7[:, 512 * m : 512 * m + 512] = moved.astype(BF16)
 
-    def taps(rows, which):
-        return sum(dot_nt(cur7[:, 512 * m : 512 * m + 512], lbuf[m, rows, :]) for m in which)
-
-    def lift_begin(i):
+    def lift(i):
         if i == 0:
             own_l.wait()
-        acc[:, :256] = taps(slice(256 * i, 256 * i + 256), range(4)) + vbl[:, 256 * i : 256 * i + 256]
-
-    def lift_end(i):
         cols = slice(256 * i, 256 * i + 256)
-        total = acc[:, :256] + taps(cols, range(4, 7))
+        total = sum(dot_nt(cur7[:, 512 * m : 512 * m + 512], lbuf[m, cols, :]) for m in range(7)) + vbl[:, cols]
         active = jnp.where(real, elu(total), 0.0).astype(BF16)
         act2[:, cols] = active
         act2[:, C0 + 256 * i : C0 + 256 * i + 256] = pltpu.roll(active.astype(F32), 1, 0).astype(BF16)
 
-    def upsample(d, half):
-        if (d, half) == (0, 0):
+    def phase(d):
+        return (g.z + d + 8) % 8
+
+    def tap(row, j, half):
+        yl = (g.y + row) % 2
+        return dot(act2[:, pl.ds(pl.multiple_of(C0 * yl, C0), C0)], ubuf[yl, j, half])
+
+    def upsample(d, units):
+        if d == 0:
             own_u.wait()
             in_c1.wait()
             in_c2.wait()
-        j = (g.z + d + 8) % 8
-        cols = slice(256 * half, 256 * half + 256)
-        up = dot(act2[:, :C0], ubuf[0, j, half]) + dot(act2[:, C0:], ubuf[1, j, half])
-        up = (up + vbu[:, cols]).astype(BF16)
-        ups[j, :, cols] = up[LEAD:]
-        rectified = jnp.where(real, elu(up.astype(F32)), 0.0)
-        rect[j + 2, :, cols] = rectified.astype(BF16)
+        for u in units:
+            residual_unit(u)
+        j = phase(d)
+        for half in range(2):
+            cols = slice(256 * half, 256 * half + 256)
+            if d == 4:
+                up = acc[:, cols] + tap(1, j, half)
+            else:
+                up = dot(act2[:, :C0], ubuf[0, j, half]) + dot(act2[:, C0:], ubuf[1, j, half])
+            up = (up + vbu[:, cols]).astype(BF16)
+            ups[j, :, cols] = up[LEAD:]
+            rectified = elu(up.astype(F32)).astype(BF16)
+            rect[j + 2, :LEAD, cols] = jnp.where(t > 0, rectified[:LEAD], BF16(0))
+            rect[j + 2, LEAD:, cols] = rectified[LEAD:]
 
         @pl.when(j >= 6)
         def _():
-            rect[j - 6, :, cols] = pltpu.roll(rectified, 1, 0).astype(BF16)
+            rect[j - 6] = pltpu.roll(rect[j + 2].astype(F32), 1, 0).astype(BF16)
 
     leaving = []
+    last_tap = {4: 2, -3: 1, -2: 0}
+
+    def conv(j, m):
+        return dot(rect[j + m, LEAD:], vc1[:, CH * m : CH * m + CH])
+
+    def last_begin(*units):
+        for u in units:
+            residual_unit(u)
+        for u, last in last_tap.items():
+            one, two = (m for m in range(3) if m != last)
+            part[last] = vb1[...] + conv(phase(u), one) + conv(phase(u), two)
+
+    def last_row():
+        for half in range(2):
+            acc[:, 256 * half : 256 * half + 256] = tap(0, phase(4), half)
 
     def residual_unit(d):
-        j = (g.z + d + 8) % 8
-        total = vb1[...]
-        for m in range(3):
-            total = total + dot(rect[j + m, LEAD:], vc1[:, CH * m : CH * m + CH])
+        j = phase(d)
+        if d in last_tap:
+            total = part[last_tap[d]] + conv(j, last_tap[d])
+        else:
+            total = vb1[...] + conv(j, 0) + conv(j, 1) + conv(j, 2)
         second = dot(elu(total).astype(BF16), vc2[...])
         obf[j] = (ups[j].astype(F32) + vb2[...] + second).astype(BF16)
         copy = pltpu.make_async_copy(obf.at[j], out.at[j], out_sems.at[len(leaving)])
         copy.start()
         leaving.append(copy)
 
+    def last_units():
+        for d in last_tap:
+            residual_unit(d)
+
     steps = dict(
         norm=first_norm, k=keys, v=values, q=queries, att=attention, post=after_attention, ff=feed_forward,
-        end=layer_end, la=lift_begin, lb=lift_end, up=upsample, ru=residual_unit,
+        end=layer_end, lift=lift, up=upsample, early=last_begin, row=last_row, last=last_units,
     )
     for name, *where in PLAN:
         if name in steps:
@@ -456,17 +500,18 @@
             vmem((LIVE, 7 * D), BF16),
             vmem((LIVE, 2 * C0), BF16),
             vmem((UPS + 2, LIVE, C1), BF16),
+            vmem((3, FRAMES, CH), F32),
             vmem((UPS, FRAMES, C1), BF16),
             vmem((UPS, FRAMES, C1), BF16),
-            dma((140,)),
-            dma((140,)),
+            dma((172,)),
+            dma((172,)),
             dma((24,)),
             dma((8,)),
         ],
         compiler_params=pltpu.CompilerParams(collective_id=0, has_side_effects=True, vmem_limit_bytes=60 * 2**20),
         cost_estimate=pl.CostEstimate(flops=11 * 10**9, bytes_accessed=36 * 10**6, transcendentals=4 * 10**6),
     )(*operands)
-    block = 64
+    block = 128
     result = pl.pallas_call(
         weave,
         out_shape=jax.ShapeDtypeStruct((FRAMES * UPS, C1), BF16),

time: 84.9 us -> 77.9 us (0.918)
  Pallas kernels: 84.8 us -> 77.8 us
    pallas_call x1, Pallas kernels: 80.4 us -> 74.2 us  [body(): pl.pallas_call(kernel, out_shape=jax.ShapeDtypeStruct((UPS, FRAMES, C1),...]
where the time goes in v3:
time: 77.9 us; the launch traced here: 77.8 us
  Pallas kernels  77.8 us (100%)
    pallas_call x1, Pallas kernels, body(): pl.pallas_call(kernel, out_shape=jax.ShapeDtypeStruct((UPS, FRAMES, C1),...  74.2 us
    pallas_call x1, Pallas kernels, body(): pl.pallas_call(weave, out_shape=jax.ShapeDtypeStruct((FRAMES * UPS, C1),...  3.62 us

profile of v3, /device:TPU:1, one launch (start us, length us, event | category | flops | bytes accessed | tf_op | source)
XLA Modules:
  0.0 77.8 jit_solution(16179119521262658620)
XLA Ops:
  0.0 74.2 %shard_map.199.phases = bf16[8,256,512]{2,1,0:T(8,128)(2,1)} custom-call(bf16[256,512]{1,0:T(8,128)(2,1)} %bitcast.19, f32[1,512]{1,0:T(1,128)} %ga.1, bf16[512,512]{1,0:T(8,128)(2,1)} %bitcast.15, bf16[512,512]{1,0:T(8,128)(2,1)} %bitcast.16, bf16[512,512]{1,0:T(8,128)(2,1)} %bitcast.17, bf16[512,512]{1,0:T(8,128)(2,1)} %bitcast.18, f32[1,512]{1,0:T(1,128)} %sa.1, ...), custom_call_target="tpu_custom_call" | custom-call | flops 11000000512 | bytes 36000000 | tf_op jit(solution)/shard_map/pallas_call | solution.py:468
  74.2 3.6 %shard_map.200 = bf16[2048,512]{1,0:T(8,128)(2,1)} custom-call(bf16[8,256,512]{2,1,0:T(8,128)(2,1)} %shard_map.199.phases), custom_call_target="tpu_custom_call" | custom-call | tf_op jit(solution)/shard_map/pallas_call | solution.py:515

commit v4 on v3

--- a/solution.py
+++ b/solution.py
@@ -179,38 +179,38 @@
 
 
 PLAN = (
-    ("L", "S", 0, 0), ("L", "M", 0, 1), ("L", "M", 1, 0), ("L", "C", 1, 0), ("norm",), ("L", "C", 0, 1),
-    ("L", "M", 0, -1), ("k",), ("L", "Oa", 1, 0), ("L", "M", 0, 2), ("L", "M", 1, 1), ("L", "O", 0, 1), ("v",),
-    ("L", "Ob", 1, 0), ("L", "C", 0, -1), ("U", "M", 0, 0), ("q",), ("L", "S", 0, 1), ("att", 0, 0), ("L", "S", 1, 0),
-    ("L", "M", 0, -2), ("L", "O", 0, -1), ("att", 0, 1), ("L", "C", 0, 2), ("L", "C", 1, 1), ("att", 0, 2),
-    ("L", "O", 0, 2), ("L", "S", 0, -1), ("L", "M", 0, 3), ("L", "M", 1, -1), ("att", 1, 0), ("L", "O", 1, 1),
-    ("L", "C", 0, -2), ("L", "C", 1, -1), ("att", 1, 1), ("L", "M", 1, 2), ("L", "S", 0, 2), ("L", "O", 0, -2),
-    ("att", 1, 2), ("L", "M", 1, -2), ("L", "S", 1, 1), ("att", 2, 0), ("L", "S", 0, -2), ("U", "M", 0, 1),
-    ("L", "O", 0, 3), ("att", 2, 1), ("L", "C", 1, 2), ("U", "M", 0, -1), ("att", 2, 2), ("U", "M", 1, 0),
-    ("L", "O", 1, -1), ("L", "C", 0, 3), ("L", "M", 1, 3), ("L", "M", 0, -3), ("att", 3, 0), ("L", "Mb", 0, 4),
-    ("L", "O", 1, 2), ("L", "O", 1, -2), ("L", "C", 1, -2), ("U", "C", 0, 0), ("L", "S", 1, -1), ("att", 3, 1),
-    ("L", "S", 0, 3), ("L", "C", 0, -3), ("att", 3, 2), ("L", "S", 1, 2), ("L", "S", 1, -2), ("post",),
-    ("U", "S", 0, 0), ("U", "M", 1, 1), ("U", "M", 0, 2), ("ff", 0), ("U", "O", 0, 1), ("L", "Mb", 1, 4),
-    ("L", "Cb", 0, 4), ("U", "M", 1, -1), ("U", "O", 0, -1), ("ff", 1), ("ff", 2), ("U", "M", 0, -2),
-    ("U", "SO", 0, 1), ("U", "Ob", 1, 0), ("ff", 3), ("U", "SO", 0, -1), ("L", "Ma", 0, 4), ("L", "Ob", 0, 4),
-    ("U", "Oa", 1, 0), ("ff", 4), ("L", "C", 1, 3), ("ff", 5), ("ff", 6), ("L", "Ob", 1, 4), ("U", "SO", 1, 0),
-    ("L", "O", 1, 3), ("L", "M", 1, -3), ("U", "C", 1, 0), ("U", "C", 0, 1), ("ff", 7), ("end",), ("L", "O", 0, -3),
-    ("L", "S", 1, 3), ("U", "C", 0, -1), ("U", "SP", 1, 0), ("L", "C", 1, -3), ("U", "SP", 0, 1), ("L", "Cb", 1, 4),
-    ("L", "S", 0, -3), ("L", "Ca", 0, 4), ("U", "O", 1, -1), ("U", "M", 1, 2), ("U", "SP", 0, -1), ("U", "M", 0, 3),
-    ("L", "Ma", 1, 4), ("U", "SO", 1, -1), ("U", "O", 1, 1), ("U", "SO", 1, 1), ("U", "M", 1, -2), ("U", "M", 0, -3),
-    ("U", "O", 0, -2), ("U", "C", 0, 2), ("U", "C", 1, 1), ("U", "SO", 0, -2), ("L", "O", 1, -3), ("U", "O", 0, 2),
-    ("U", "SP", 0, 2), ("L", "Oa", 0, 4), ("U", "Mb", 0, 4), ("L", "Ca", 1, 4), ("U", "SP", 1, 1), ("L", "Oa", 1, 4),
-    ("L", "S", 1, -3), ("U", "C", 1, -1), ("U", "SO", 0, 2), ("U", "C", 0, -2), ("L", "S", 0, 4), ("L", "S", 1, 4),
-    ("lift", 0), ("U", "O", 1, 2), ("U", "SP", 1, -1), ("lift", 1), ("U", "Ma", 0, 4), ("U", "SP", 0, -2),
-    ("lift", 2), ("U", "M", 1, -3), ("U", "SO", 1, 2), ("U", "O", 1, -2), ("U", "C", 0, 3), ("U", "M", 1, 3),
-    ("lift", 3), ("up", 0, ()), ("U", "SO", 1, -2), ("U", "O", 0, 3), ("U", "SP", 0, 3), ("up", -1, ()),
-    ("U", "C", 0, -3), ("U", "C", 1, -2), ("U", "SO", 0, 3), ("U", "O", 0, -3), ("U", "Ob", 0, 4), ("up", 1, ()),
-    ("U", "C", 1, 2), ("U", "Cb", 0, 4), ("U", "SP", 0, -3), ("U", "Ma", 1, 4), ("U", "Oa", 0, 4), ("U", "SP", 1, -2),
-    ("up", -2, (1,)), ("U", "Mb", 1, 4), ("U", "SO", 0, -3), ("U", "SP", 1, 2), ("U", "SO", 0, 4), ("U", "O", 1, -3),
-    ("up", 2, (0,)), ("U", "Ca", 0, 4), ("U", "SO", 1, -3), ("U", "C", 1, 3), ("U", "O", 1, 3), ("U", "C", 1, -3),
-    ("U", "SP", 0, 4), ("U", "Oa", 1, 4), ("U", "SP", 1, 3), ("U", "Ob", 1, 4), ("U", "SO", 1, 3), ("U", "Cb", 1, 4),
-    ("U", "SP", 1, -3), ("up", -3, (2,)), ("U", "SO", 1, 4), ("U", "Ca", 1, 4), ("up", 3, (-1,)), ("U", "SP", 1, 4),
-    ("early", 3), ("row",), ("up", 4, ()), ("last",),
+    ("L", "S", 0, 0), ("L", "M", 0, -1), ("L", "M", 0, 1), ("L", "M", 1, 0), ("L", "C", 1, 0), ("L", "C", 0, -1),
+    ("U", "M", 0, 0), ("L", "C", 0, 1), ("L", "M", 1, -1), ("L", "O", 0, -1), ("L", "M", 0, 2), ("L", "M", 1, 1),
+    ("L", "O", 0, 1), ("L", "Oa", 1, 0), ("L", "Ob", 1, 0), ("L", "S", 0, -1), ("L", "S", 0, 1), ("L", "S", 1, 0),
+    ("norm",), ("L", "C", 1, -1), ("L", "O", 1, -1), ("L", "M", 0, -2), ("L", "O", 0, 2), ("k",), ("U", "M", 0, 1),
+    ("U", "M", 1, 0), ("L", "S", 1, -1), ("L", "O", 1, 1), ("v",), ("L", "C", 0, -2), ("q",), ("L", "C", 0, 2),
+    ("L", "C", 1, 1), ("att", 0, 0), ("L", "M", 1, -2), ("L", "O", 0, -2), ("L", "M", 0, 3), ("L", "M", 1, 2),
+    ("att", 0, 1), ("L", "S", 0, 2), ("L", "S", 1, 1), ("att", 0, 2), ("L", "S", 0, -2), ("U", "M", 0, -1),
+    ("U", "Oa", 1, 0), ("att", 1, 0), ("L", "C", 1, -2), ("U", "C", 0, 0), ("L", "M", 0, -3), ("att", 1, 1),
+    ("U", "M", 1, 1), ("U", "O", 0, 1), ("U", "M", 0, 2), ("L", "O", 1, -2), ("att", 1, 2), ("U", "S", 0, 0),
+    ("L", "C", 0, -3), ("att", 2, 0), ("U", "Ob", 1, 0), ("U", "SO", 0, 1), ("L", "C", 1, 2), ("L", "C", 0, 3),
+    ("L", "S", 1, -2), ("att", 2, 1), ("L", "Mb", 0, 4), ("L", "O", 0, 3), ("L", "M", 1, 3), ("U", "SO", 1, 0),
+    ("att", 2, 2), ("U", "M", 1, -1), ("L", "O", 1, 2), ("U", "O", 0, -1), ("att", 3, 0), ("L", "S", 0, 3),
+    ("U", "M", 0, -2), ("att", 3, 1), ("L", "M", 1, -3), ("L", "O", 0, -3), ("L", "S", 1, 2), ("U", "SO", 0, -1),
+    ("U", "C", 0, 1), ("L", "Ob", 0, 4), ("att", 3, 2), ("U", "C", 1, 0), ("post",), ("L", "S", 0, -3), ("ff", 0),
+    ("U", "SP", 0, 1), ("ff", 1), ("U", "C", 0, -1), ("U", "SP", 1, 0), ("L", "C", 1, -3), ("U", "M", 1, 2),
+    ("U", "O", 1, 1), ("L", "Ma", 0, 4), ("ff", 2), ("L", "Mb", 1, 4), ("U", "M", 0, 3), ("ff", 3), ("U", "O", 1, -1),
+    ("L", "Cb", 0, 4), ("U", "SP", 0, -1), ("L", "Ca", 0, 4), ("ff", 4), ("U", "SO", 1, 1), ("L", "C", 1, 3),
+    ("ff", 5), ("ff", 6), ("U", "SO", 1, -1), ("ff", 7), ("end",), ("U", "O", 0, 2), ("U", "M", 1, -2),
+    ("U", "O", 0, -2), ("L", "O", 1, 3), ("U", "M", 0, -3), ("U", "C", 0, 2), ("U", "SO", 0, 2), ("L", "Oa", 0, 4),
+    ("U", "C", 1, 1), ("U", "SO", 0, -2), ("L", "O", 1, -3), ("L", "S", 1, 3), ("L", "Ma", 1, 4), ("U", "Mb", 0, 4),
+    ("U", "SP", 0, 2), ("L", "S", 0, 4), ("U", "C", 1, -1), ("L", "Ca", 1, 4), ("U", "SP", 1, 1), ("L", "S", 1, -3),
+    ("U", "C", 0, -2), ("U", "SP", 1, -1), ("U", "O", 1, 2), ("U", "O", 1, -2), ("L", "Ob", 1, 4), ("U", "SP", 0, -2),
+    ("U", "Ma", 0, 4), ("U", "SO", 1, 2), ("U", "SO", 1, -2), ("U", "C", 0, 3), ("U", "M", 1, 3), ("U", "M", 1, -3),
+    ("L", "Cb", 1, 4), ("U", "SP", 0, 3), ("U", "O", 0, -3), ("U", "O", 0, 3), ("L", "Oa", 1, 4), ("U", "SO", 0, -3),
+    ("U", "C", 0, -3), ("U", "C", 1, -2), ("U", "SO", 0, 3), ("U", "Ob", 0, 4), ("U", "Cb", 0, 4), ("L", "S", 1, 4),
+    ("lift", 0), ("U", "C", 1, 2), ("U", "Oa", 0, 4), ("lift", 1), ("U", "SP", 0, -3), ("U", "Ma", 1, 4),
+    ("U", "SP", 1, -2), ("lift", 2), ("U", "Mb", 1, 4), ("U", "SP", 1, 2), ("lift", 3), ("U", "SO", 0, 4),
+    ("up", 0, ()), ("U", "O", 1, -3), ("U", "Ca", 0, 4), ("U", "O", 1, 3), ("up", -1, ()), ("U", "C", 1, 3),
+    ("U", "SO", 1, -3), ("U", "C", 1, -3), ("up", 1, ()), ("U", "Oa", 1, 4), ("U", "SP", 0, 4), ("U", "SO", 1, 3),
+    ("U", "Ob", 1, 4), ("up", -2, (1,)), ("U", "SP", 1, 3), ("U", "Cb", 1, 4), ("U", "SP", 1, -3), ("U", "SO", 1, 4),
+    ("U", "Ca", 1, 4), ("up", 2, (0,)), ("U", "SP", 1, 4), ("up", -3, (2,)), ("up", 3, (-1,)), ("early", 3), ("row",),
+    ("up", 4, ()), ("last",),
 )
 
 
@@ -252,10 +252,10 @@
     own_x = bring(lat, xin.at[pl.ds(HALO, FRAMES)])
     in_ga, in_near, in_far = bring(ga, vga), bring(near, vnear), bring(far, vfar)
     g.barrier()
+    g.event("L", "M", 0, 0)
+    g.event("L", "C", 0, 0)
     g.start(lat, xin.at[pl.ds(LEAD, FRAMES)], g.after[0], 0)
     g.start(lat.at[pl.ds(FRAMES - LEAD, LEAD)], xin.at[pl.ds(0, LEAD)], g.after[1], 1)
-    g.event("L", "M", 0, 0)
-    g.event("L", "C", 0, 0)
     in_proj = [bring(w, vproj.at[i]) for i, w in enumerate((wk, wv, wq, wo))]
     own_l = bring(wl, g.ref("L", "W", 0, 0))
     own_u = bring(wu, g.ref("U", "W", 0, 0))

time: 77.9 us -> 82.3 us (1.056)
  Pallas kernels: 77.8 us -> 82.2 us
    pallas_call x1, Pallas kernels: 74.2 us -> 78.6 us  [body(): pl.pallas_call(kernel, out_shape=jax.ShapeDtypeStruct((UPS, FRAMES, C1),...]
where the time goes in v4:
time: 82.3 us; the launch traced here: 82.2 us
  Pallas kernels  82.2 us (100%)
    pallas_call x1, Pallas kernels, body(): pl.pallas_call(kernel, out_shape=jax.ShapeDtypeStruct((UPS, FRAMES, C1),...  78.6 us
    pallas_call x1, Pallas kernels, body(): pl.pallas_call(weave, out_shape=jax.ShapeDtypeStruct((FRAMES * UPS, C1),...  3.62 us

profile of v4, /device:TPU:1, one launch (start us, length us, event | category | flops | bytes accessed | tf_op | source)
XLA Modules:
  0.0 82.2 jit_solution(7309181640485447038)
XLA Ops:
  0.0 78.6 %shard_map.199.phases = bf16[8,256,512]{2,1,0:T(8,128)(2,1)} custom-call(bf16[256,512]{1,0:T(8,128)(2,1)} %bitcast.19, f32[1,512]{1,0:T(1,128)} %ga.1, bf16[512,512]{1,0:T(8,128)(2,1)} %bitcast.15, bf16[512,512]{1,0:T(8,128)(2,1)} %bitcast.16, bf16[512,512]{1,0:T(8,128)(2,1)} %bitcast.17, bf16[512,512]{1,0:T(8,128)(2,1)} %bitcast.18, f32[1,512]{1,0:T(1,128)} %sa.1, ...), custom_call_target="tpu_custom_call" | custom-call | flops 11000000512 | bytes 36000000 | tf_op jit(solution)/shard_map/pallas_call | solution.py:468
  78.6 3.6 %shard_map.200 = bf16[2048,512]{1,0:T(8,128)(2,1)} custom-call(bf16[8,256,512]{2,1,0:T(8,128)(2,1)} %shard_map.199.phases), custom_call_target="tpu_custom_call" | custom-call | tf_op jit(solution)/shard_map/pallas_call | solution.py:515
